TPU v7x, 128 devices: a whole 4x4x4 slice. The times are simulated.
128 devices in a mesh: row: 8 (over y, core), col: 16 (over z, x).
Axes of the slice: x: 4, y: 4, z: 4, core: 2. Of those that a mesh axis runs over, the one named last changes fastest.
Arguments:
- obs_jac: bfloat16 [4096, 2, 1024, 128], P(('row', 'col')), may hold values from -0.1265625 to 0.1265625
- rad_jac: float32 [4096, 2, 1024], P(('row', 'col')), may hold values from -4 to 4
- obs_residual: float32 [4096, 2, 1024], P(('row', 'col')), may hold values from -6 to 6
- track_damping: float32 [4096, 1024], P(('row', 'col')), may hold values from 0.2 to 5
- track_block_column: int32 [4096, 1], P(('row', 'col')), may hold values from 0 to 15; in each aligned block of 32 rows (0 to 31, 32 to 63, ...) at most 3 rows name the same one
- track_slot: int32 [4096], P(('row', 'col')), may hold values from 0 to 31
- pair_rows: int32 [4096], P(('row', 'col')), may hold values from 0 to 255
- pair_cols: int32 [4096], P(('row', 'col')), may hold values from 0 to 127
- image_damping: float32 [2048, 128], P(('row', 'col')), may hold values from 0.1 to 2
Outputs:
- update: float32 [2048, 128], P(('row', 'col'))
- residual: float32 [2048, 128], P(('row', 'col'))
Inputs may be any that keep to these rules, and one draw needn't show every extreme that they name: `track_block_column`: among the track blocks of one device, at most 3 name the same block column; some device has exactly 3 for some column.
All inputs are finite; a program needn't handle non-finite values.
Results may differ from a plain program's by a relative error of at most 0.02.
Values may be sent and summed in bfloat16 or wider, within the bound.
A program may use at most 192 MiB of HBM per device.

v0:
```python
import jax
import jax.numpy as jnp
from jax import lax
from jax.sharding import PartitionSpec as P

ITERS = 3


def coefficients(rad, resid, damp):
    first_h = rad[..., 0, :]
    second_h = rad[..., 1, :]
    first_e = resid[..., 0, :]
    second_e = resid[..., 1, :]
    total = first_h * first_h + second_h * second_h + damp
    track_grad = first_h * first_e + second_h * second_e
    track_coefficient = jnp.stack(
        [
            1.0 - first_h * first_h / total,
            1.0 - second_h * second_h / total,
            -first_h * second_h / total,
            first_e - first_h * track_grad / total,
            second_e - second_h * track_grad / total,
        ],
        axis=-2,
    )
    return track_coefficient.astype(jnp.bfloat16)


def row_scale_factors(coef_row, matrix):
    return (coef_row[:, :, None].astype(jnp.float32) * matrix).astype(jnp.bfloat16)


def form_terms(jac, track_coefficient):
    first_image = jac[:, 0]
    second_image = jac[:, 1]
    block_aa = jnp.einsum(
        "xhb,xhu->xbu",
        first_image,
        row_scale_factors(track_coefficient[:, 0], first_image),
        preferred_element_type=jnp.float32,
    ).astype(jnp.bfloat16)
    block_bb = jnp.einsum(
        "xhb,xhu->xbu",
        second_image,
        row_scale_factors(track_coefficient[:, 1], second_image),
        preferred_element_type=jnp.float32,
    ).astype(jnp.bfloat16)
    block_ab = jnp.einsum(
        "xhb,xhu->xbu",
        first_image,
        row_scale_factors(track_coefficient[:, 2], second_image),
        preferred_element_type=jnp.float32,
    ).astype(jnp.bfloat16)
    blocks = jnp.stack([block_aa, block_bb, block_ab], axis=1)
    vectors = jnp.einsum(
        "kjt,kjtp->kjp", track_coefficient[:, 3:], jac, preferred_element_type=jnp.float32
    ).astype(jnp.bfloat16)
    return (blocks, vectors)


def shards(
    obs_jac,
    rad_jac,
    obs_residual,
    track_damping,
    track_block_column,
    track_slot,
    pair_rows,
    pair_cols,
    image_damping,
):
    highest = lax.Precision.HIGHEST
    columns = lax.axis_size("col")
    rows_count = lax.axis_size("row")
    blocks_here = obs_jac.shape[0]
    capacity = 3 * blocks_here // (2 * columns)
    slot_count = columns * capacity
    pairs = pair_rows.shape[0]
    own_images = image_damping.shape[0]
    row_images = own_images * columns
    col_images = own_images * rows_count
    destination = track_block_column[:, 0]
    ordinal = jnp.arange(blocks_here, dtype=jnp.int32)
    same_target = destination[:, None] == destination[None, :]
    earlier = ordinal[:, None] > ordinal[None, :]
    position = jnp.sum(jnp.logical_and(same_target, earlier), axis=1)
    target = destination * capacity + position
    send_slots = jnp.full((slot_count,), -1, jnp.int32).at[target].set(track_slot)
    track_coefficient = coefficients(rad_jac, obs_residual, track_damping)
    local_blocks, local_vectors = form_terms(obs_jac, track_coefficient)
    send_blocks = (
        jnp.zeros((slot_count,) + local_blocks.shape[1:], jnp.bfloat16).at[target].set(local_blocks)
    )
    outgoing_vectors = (
        jnp.zeros((slot_count,) + local_vectors.shape[1:], jnp.bfloat16)
        .at[target]
        .set(local_vectors)
    )
    blocks, vectors, recv_slots = (
        lax.all_to_all(send_blocks, "col", split_axis=0, concat_axis=0, tiled=True),
        lax.all_to_all(outgoing_vectors, "col", split_axis=0, concat_axis=0, tiled=True),
        lax.all_to_all(send_slots, "col", split_axis=0, concat_axis=0, tiled=True),
    )
    pair_hot = (recv_slots[None, :] == jnp.arange(pairs, dtype=jnp.int32)[:, None]).astype(
        jnp.bfloat16
    )
    pair_blocks = jnp.einsum("ps,sjab->pjab", pair_hot, blocks, preferred_element_type=jnp.float32)
    pair_vectors = jnp.einsum("ps,sja->pja", pair_hot, vectors, preferred_element_type=jnp.float32)
    row_hot = (pair_rows[None, :] == jnp.arange(row_images, dtype=jnp.int32)[:, None]).astype(
        jnp.float32
    )
    col_hot = (pair_cols[None, :] == jnp.arange(col_images, dtype=jnp.int32)[:, None]).astype(
        jnp.float32
    )
    first_diag = jnp.diagonal(pair_blocks[:, 0], axis1=1, axis2=2)
    second_diag = jnp.diagonal(pair_blocks[:, 1], axis1=1, axis2=2)
    row_rhs = jnp.dot(row_hot, pair_vectors[:, 0], precision=highest)
    row_diag = jnp.dot(row_hot, first_diag, precision=highest)
    col_rhs = jnp.dot(col_hot, pair_vectors[:, 1], precision=highest)
    col_diag = jnp.dot(col_hot, second_diag, precision=highest)
    rhs_first, diag_first = (
        lax.psum_scatter(row_rhs, "col", scatter_dimension=0, tiled=True),
        lax.psum_scatter(row_diag, "col", scatter_dimension=0, tiled=True),
    )
    rhs_second, diag_second = (
        lax.psum_scatter(col_rhs, "row", scatter_dimension=0, tiled=True),
        lax.psum_scatter(col_diag, "row", scatter_dimension=0, tiled=True),
    )
    right_side = rhs_first + rhs_second
    diagonal = image_damping + diag_first + diag_second

    def precond_inner(left, right):
        return lax.psum(jnp.sum(left * right), ("row", "col"))

    update = jnp.zeros_like(right_side)
    residual = right_side
    scaled = residual / diagonal
    direction = scaled
    inner_now = precond_inner(residual, scaled)
    for iteration in range(ITERS):
        row_field = lax.all_gather(direction, "col", axis=0, tiled=True)
        col_field = lax.all_gather(direction, "row", axis=0, tiled=True)
        first_in = jnp.dot(row_hot.T, row_field, precision=highest)
        second_in = jnp.dot(col_hot.T, col_field, precision=highest)
        first_out = jnp.einsum("pab,pb->pa", pair_blocks[:, 0], first_in, precision=highest)
        first_out = first_out + jnp.einsum(
            "pab,pb->pa", pair_blocks[:, 2], second_in, precision=highest
        )
        second_out = jnp.einsum("pab,pb->pa", pair_blocks[:, 1], second_in, precision=highest)
        second_out = second_out + jnp.einsum(
            "pba,pb->pa", pair_blocks[:, 2], first_in, precision=highest
        )
        row_part = jnp.dot(row_hot, first_out, precision=highest)
        col_part = jnp.dot(col_hot, second_out, precision=highest)
        result = image_damping * direction + lax.psum_scatter(
            row_part, "col", scatter_dimension=0, tiled=True
        )
        image = result + lax.psum_scatter(col_part, "row", scatter_dimension=0, tiled=True)
        step_length = inner_now / lax.psum(jnp.sum(direction * image), ("row", "col"))
        update = update + step_length * direction
        residual = residual - step_length * image
        scaled = residual / diagonal
        inner_next = precond_inner(residual, scaled)
        direction = scaled + inner_next / inner_now * direction
        inner_now = inner_next
    return (update, residual)


def solution(mesh):
    in_specs = (
        P(("row", "col"), None, None, None),
        P(("row", "col"), None, None),
        P(("row", "col"), None, None),
        P(("row", "col"), None),
        P(("row", "col"), None),
        P(("row", "col")),
        P(("row", "col")),
        P(("row", "col")),
        P(("row", "col"), None),
    )
    out_specs = (P(("row", "col"), None), P(("row", "col"), None))
    return jax.shard_map(shards, mesh=mesh, in_specs=in_specs, out_specs=out_specs, check_vma=False)
```

profile of v0, /device:TPU:1, one launch (start us, length us, event | category | flops | bytes accessed | tf_op | source)
XLA Modules:
  0.0 1039.4 jit_solution(3190908957397891608)
XLA Ops:
  8.0 0.9 convert_reduce_fusion
  11.1 8.4 all-to-all-start
  19.5 1.7 fusion.130
  21.2 1.2 fusion.93
  22.5 12.7 %fusion.59 = bf16[32,1,128,128]{2,3,0,1:T(8,128)(2,1)S(1)} fusion(bf16[32,2,1024,128]{3,2,1,0:T(8,128)(2,1)} %param.9, f32[32,1024]{1,0:T(8,128)S(1)} %get-tuple-element.29), kind=kOutput, calls=%fused_computation.53 | convolution fusion | flops 1086849024 | bytes 17956864 | tf_op jit(solution)/shard_map/xhb,xhu->xbu/dot_general | solution.py:48
  35.3 12.7 %fusion.54 = bf16[32,1,128,128]{2,3,0,1:T(8,128)(2,1)S(1)} fusion(bf16[32,2,1024,128]{3,2,1,0:T(8,128)(2,1)S(1)} %bitcast.227, f32[32,1024]{1,0:T(8,128)S(1)} %get-tuple-element.28), kind=kOutput, calls=%fused_computation.52 | convolution fusion | flops 1086849024 | bytes 17956864 | tf_op jit(solution)/shard_map/xhb,xhu->xbu/dot_general | solution.py:42
  48.0 13.4 %fusion.51 = bf16[32,1,128,128]{2,3,0,1:T(8,128)(2,1)} fusion(bf16[32,2,1024,128]{3,2,1,0:T(8,128)(2,1)S(1)} %bitcast.227, f32[32,1024]{1,0:T(8,128)S(1)} %get-tuple-element.27), kind=kOutput, calls=%fused_computation.51 | convolution fusion | flops 1086849024 | bytes 17956864 | tf_op jit(solution)/shard_map/xhb,xhu->xbu/dot_general | solution.py:36
  61.4 2.3 fusion.64
  64.3 3.9 scatter_fusion
  68.3 6.6 all-to-all-start.1
  74.9 3.3 pad_maximum_fusion
  78.1 4.6 copy.62
  82.8 3.3 broadcast_in_dim.12
  86.1 10.4 scatter_fusion.1
  96.5 6.8 all-to-all-start.2
  105.9 0.8 fusion.73
  106.7 63.6 %all-to-all-done.2 = bf16[48,3,128,128]{3,2,1,0:T(8,128)(2,1)} async-done(((bf16[48,3,128,128]{3,2,1,0:T(8,128)(2,1)}), bf16[48,3,128,128]{3,2,1,0:T(8,128)(2,1)}, u32[]{:S(2)}, u32[]{:S(2)}) %all-to-all-start.2) | async-done | bytes 4718624 | tf_op jit(solution)/shard_map/all_to_all | solution.py:100
  170.3 5.7 fusion.18
  176.0 2.6 slice_bitcast_fusion
  178.6 4.7 copy.65
  183.3 6.2 copy.64
  189.5 1.8 gather_fusion.1
  191.3 1.8 gather_fusion
  193.1 0.8 fusion.80
  194.0 0.9 fusion.72
  196.2 3.0 copy.80
  199.2 24.0 %reduce-scatter.8.cloned.1.call-done = f32[16,128]{1,0:T(8,128)} async-done(((f32[128,128]{1,0:T(8,128)}), f32[16,128]{1,0:T(8,128)}) %reduce-scatter.8.cloned.1.call-update) | async-done | bytes 8208 | tf_op jit(solution)/shard_map/reduce_scatter | solution.py:127
  223.3 58.1 %all-reduce.18.cloned.1.call-done = (f32[256,128]{1,0:T(8,128)}, f32[256,128]{1,0:T(8,128)}) async-done(((f32[256,128]{1,0:T(8,128)}, f32[256,128]{1,0:T(8,128)}), (f32[256,128]{1,0:T(8,128)}, f32[256,128]{1,0:T(8,128)})) %all-reduce.18.cloned.1.call-update) | async-done | bytes 262160
  281.4 0.9 fusion.128
  282.3 15.4 %all_gather.19 = f32[128,128]{1,0:T(8,128)S(1)} all-gather(f32[16,128]{1,0:T(8,128)S(1)} %get-tuple-element.19), channel_id=1, replica_groups=mesh['row'=8,'col'=16] {'row'}, dimensions={0}, use_global_device_ids=true | all-gather | bytes 73728 | tf_op jit(solution)/shard_map/all_gather | solution.py:142
  297.7 17.8 %all_gather.18 = f32[256,128]{1,0:T(8,128)S(1)} all-gather(f32[16,128]{1,0:T(8,128)S(1)} %get-tuple-element.19), channel_id=1, replica_groups=mesh['row'=8,'col'=16] {'col'}, dimensions={0}, use_global_device_ids=true | all-gather | bytes 139264 | tf_op jit(solution)/shard_map/all_gather | solution.py:141
  315.8 4.4 fusion.24
  320.2 5.9 fusion.28
  326.4 4.4 fusion.36
  330.8 3.5 fusion.132
  335.1 0.8 fusion.70
  336.1 29.8 %reduce-scatter.10.cloned.1.call-done = f32[16,128]{1,0:T(8,128)} async-done(((f32[128,128]{1,0:T(8,128)}), f32[16,128]{1,0:T(8,128)}) %reduce-scatter.10.cloned.1.call-update) | async-done | bytes 8208 | tf_op jit(solution)/shard_map/reduce_scatter | solution.py:158
  365.9 56.0 %all-reduce.12.cloned.1.call-done = f32[256,128]{1,0:T(8,128)} async-done(((f32[256,128]{1,0:T(8,128)}), f32[256,128]{1,0:T(8,128)}) %all-reduce.12.cloned.1.call-update) | async-done | bytes 131088
  421.9 1.3 multiply_reduce_fusion.4
  423.2 65.9 %all-reduce.5 = (f32[]{:T(128)}, f32[]{:T(128)}) all-reduce(f32[]{:T(128)} %get-tuple-element.3, f32[]{:T(128)} %get-tuple-element.2), channel_id=1, replica_groups=mesh['row'=8,'col'=16] {'row','col'}, use_global_device_ids=true, to_apply=%region_9.10 | all-reduce | flops 2 | bytes 16 | tf_op jit(solution)/shard_map/psum | solution.py:133
  491.1 62.5 %psum.44 = f32[]{:T(128)} all-reduce(f32[]{:T(128)} %get-tuple-element.15), channel_id=1, replica_groups=mesh['row'=8,'col'=16] {'row','col'}, use_global_device_ids=true, to_apply=%region_15.16 | all-reduce | flops 1 | bytes 8 | tf_op jit(solution)/shard_map/psum | solution.py:133
  555.0 13.3 %all_gather.21 = f32[128,128]{1,0:T(8,128)S(1)} all-gather(f32[16,128]{1,0:T(8,128)S(1)} %multiply_add_fusion.3), channel_id=1, replica_groups=mesh['row'=8,'col'=16] {'row'}, dimensions={0}, use_global_device_ids=true | all-gather | bytes 73728 | tf_op jit(solution)/shard_map/all_gather | solution.py:142
  568.3 18.0 %all_gather.20 = f32[256,128]{1,0:T(8,128)S(1)} all-gather(f32[16,128]{1,0:T(8,128)S(1)} %multiply_add_fusion.3), channel_id=1, replica_groups=mesh['row'=8,'col'=16] {'col'}, dimensions={0}, use_global_device_ids=true | all-gather | bytes 139264 | tf_op jit(solution)/shard_map/all_gather | solution.py:141
  586.6 5.1 fusion.133
  591.7 4.4 fusion.34
  596.3 4.4 fusion.22
  600.7 4.6 fusion.30
  606.2 0.8 fusion.68
  607.1 28.5 %reduce-scatter.12.cloned.1.call-done = f32[16,128]{1,0:T(8,128)} async-done(((f32[128,128]{1,0:T(8,128)}), f32[16,128]{1,0:T(8,128)}) %reduce-scatter.12.cloned.1.call-update) | async-done | bytes 8208 | tf_op jit(solution)/shard_map/reduce_scatter | solution.py:158
  635.6 56.0 %all-reduce.14.cloned.1.call-done = f32[256,128]{1,0:T(8,128)} async-done(((f32[256,128]{1,0:T(8,128)}), f32[256,128]{1,0:T(8,128)}) %all-reduce.14.cloned.1.call-update) | async-done | bytes 131088
  691.7 1.3 multiply_reduce_fusion.2
  693.0 66.0 %psum.45 = f32[]{:T(128)} all-reduce(f32[]{:T(128)} %get-tuple-element.13), channel_id=1, replica_groups=mesh['row'=8,'col'=16] {'row','col'}, use_global_device_ids=true, to_apply=%region_19.20 | all-reduce | flops 1 | bytes 8 | tf_op jit(solution)/shard_map/psum | solution.py:159
  760.9 62.5 %psum.46 = f32[]{:T(128)} all-reduce(f32[]{:T(128)} %get-tuple-element.10), channel_id=1, replica_groups=mesh['row'=8,'col'=16] {'row','col'}, use_global_device_ids=true, to_apply=%region_21.22 | all-reduce | flops 1 | bytes 8 | tf_op jit(solution)/shard_map/psum | solution.py:133
  824.8 13.3 %all_gather.23 = f32[128,128]{1,0:T(8,128)S(1)} all-gather(f32[16,128]{1,0:T(8,128)S(1)} %multiply_add_fusion.2), channel_id=1, replica_groups=mesh['row'=8,'col'=16] {'row'}, dimensions={0}, use_global_device_ids=true | all-gather | bytes 73728 | tf_op jit(solution)/shard_map/all_gather | solution.py:142
  838.1 18.0 %all_gather.22 = f32[256,128]{1,0:T(8,128)S(1)} all-gather(f32[16,128]{1,0:T(8,128)S(1)} %multiply_add_fusion.2), channel_id=1, replica_groups=mesh['row'=8,'col'=16] {'col'}, dimensions={0}, use_global_device_ids=true | all-gather | bytes 139264 | tf_op jit(solution)/shard_map/all_gather | solution.py:141
  856.4 5.1 fusion.134
  861.5 4.4 fusion.32
  866.1 4.4 fusion.20
  870.5 4.6 fusion.26
  876.0 0.9 fusion.66
  876.9 28.6 %reduce-scatter.14.cloned.1.call-done = f32[16,128]{1,0:T(8,128)} async-done(((f32[128,128]{1,0:T(8,128)}), f32[16,128]{1,0:T(8,128)}) %reduce-scatter.14.cloned.1.call-update) | async-done | bytes 8208 | tf_op jit(solution)/shard_map/reduce_scatter | solution.py:158
  905.4 56.3 %all-reduce.16.cloned.1.call-done = f32[256,128]{1,0:T(8,128)} async-done(((f32[256,128]{1,0:T(8,128)}), f32[256,128]{1,0:T(8,128)}) %all-reduce.16.cloned.1.call-update) | async-done | bytes 131088
  961.8 1.3 multiply_reduce_fusion
  963.1 66.0 %psum.47 = f32[]{:T(128)} all-reduce(f32[]{:T(128)} %get-tuple-element.8), channel_id=1, replica_groups=mesh['row'=8,'col'=16] {'row','col'}, use_global_device_ids=true, to_apply=%region_25.26 | all-reduce | flops 1 | bytes 8 | tf_op jit(solution)/shard_map/psum | solution.py:159
  (78 shorter events, 12.7 us)
Async XLA Ops:
  11.1 57.2 %all-to-all-start = ((s32[16,3,1]{1,2,0:T(1,128)}), s32[16,3,1]{1,2,0:T(1,128)S(1)}, u32[]{:S(2)}, u32[]{:S(2)}) async-start(s32[16,3,1]{1,2,0:T(1,128)} %bitcast.3), calls=%async_computation | async-start | bytes 16384 | tf_op jit(solution)/shard_map/all_to_all | solution.py:102
  21.2 14.0 %slice-start = ((s8[16777216]{0:T(1024)(128)(4,1)}), s8[4194304]{0:T(1024)(128)(4,1)S(1)}, s32[]{:S(2)}) async-start(s8[16777216]{0:T(1024)(128)(4,1)} %bitcast.226), calls=%async_computation.17 | async-start | bytes 8388608
  22.4 12.8 %slice-start.1 = ((s8[16777216]{0:T(1024)(128)(4,1)}), s8[4194304]{0:T(1024)(128)(4,1)S(1)}, s32[]{:S(2)}) async-start(s8[16777216]{0:T(1024)(128)(4,1)} %bitcast.226), calls=%async_computation.18 | async-start | bytes 8388608
  22.5 12.8 %slice-start.2 = ((s8[16777216]{0:T(1024)(128)(4,1)}), s8[4194304]{0:T(1024)(128)(4,1)S(1)}, s32[]{:S(2)}) async-start(s8[16777216]{0:T(1024)(128)(4,1)} %bitcast.226), calls=%async_computation.19 | async-start | bytes 8388608
  22.5 12.8 %slice-start.3 = ((s8[16777216]{0:T(1024)(128)(4,1)}), s8[4194304]{0:T(1024)(128)(4,1)S(1)}, s32[]{:S(2)}) async-start(s8[16777216]{0:T(1024)(128)(4,1)} %bitcast.226), calls=%async_computation.20 | async-start | bytes 8388608
  68.3 28.2 %all-to-all-start.1 = ((bf16[48,2,128]{2,1,0:T(2,128)(2,1)}), bf16[48,2,128]{2,1,0:T(2,128)(2,1)S(1)}, u32[]{:S(2)}, u32[]{:S(2)}) async-start(bf16[48,2,128]{2,1,0:T(2,128)(2,1)} %scatter_fusion), calls=%async_computation.1 | async-start | bytes 49152 | tf_op jit(solution)/shard_map/all_to_all | solution.py:101
  96.5 8.3 copy-start.7
  96.5 9.4 copy-start.8
  96.5 73.8 %all-to-all-start.2 = ((bf16[48,3,128,128]{3,2,1,0:T(8,128)(2,1)}), bf16[48,3,128,128]{3,2,1,0:T(8,128)(2,1)}, u32[]{:S(2)}, u32[]{:S(2)}) async-start(bf16[48,3,128,128]{3,2,1,0:T(8,128)(2,1)} %scatter_fusion.1), calls=%async_computation.3 | async-start | bytes 9437184 | tf_op jit(solution)/shard_map/all_to_all | solution.py:100
  103.3 95.9 %reduce-scatter.6.cloned.1.call-start = ((), (), s32[]{:S(2)}) async-start(), calls=%async_computation.8 | async-start | bytes 73728 | tf_op jit(solution)/shard_map/reduce_scatter | solution.py:126
  105.6 117.7 %reduce-scatter.8.cloned.1.call-start = ((), (), s32[]{:S(2)}) async-start(), calls=%async_computation.9 | async-start | bytes 73728 | tf_op jit(solution)/shard_map/reduce_scatter | solution.py:127
  183.3 11.7 %copy-start.9 = (u32[128]{0:T(128)S(1)}, u32[128]{0:T(128)}, u32[]{:S(2)}) copy-start(u32[128]{0:T(128)} %constant.60) | copy-start | bytes 1540
  189.5 91.9 %copy-start.6 = (f32[16,128]{1,0:T(8,128)S(1)}, f32[16,128]{1,0:T(8,128)}, u32[]{:S(2)}) copy-start(f32[16,128]{1,0:T(8,128)} %param.17) | copy-start | bytes 24580
  194.0 87.5 %all-reduce.18.cloned.1.call-start = ((), (), s32[]{:S(2)}) async-start(), calls=%async_computation.16 | async-start | bytes 524288
  194.9 171.0 %reduce-scatter.10.cloned.1.call-start = ((), (), s32[]{:S(2)}) async-start(), calls=%async_computation.10 | async-start | bytes 73728 | tf_op jit(solution)/shard_map/reduce_scatter | solution.py:158
  281.4 44.9 %copy-start = (f32[32,128,128]{2,0,1:T(8,128)S(1)}, f32[32,128,128]{2,0,1:T(8,128)}, u32[]{:S(2)}) copy-start(f32[32,128,128]{2,0,1:T(8,128)} %get-tuple-element.24) | copy-start | bytes 6291460
  315.8 15.0 %copy-start.5 = (f32[32,128,128]{1,2,0:T(8,128)S(1)}, f32[32,128,128]{1,2,0:T(8,128)}, u32[]{:S(2)}) copy-start(f32[32,128,128]{1,2,0:T(8,128)} %copy.80) | copy-start | bytes 6291460
  335.1 86.8 %all-reduce.12.cloned.1.call-start = ((), (), s32[]{:S(2)}) async-start(), calls=%async_computation.13 | async-start | bytes 262144
  336.0 299.6 %reduce-scatter.12.cloned.1.call-start = ((), (), s32[]{:S(2)}) async-start(), calls=%async_computation.11 | async-start | bytes 73728 | tf_op jit(solution)/shard_map/reduce_scatter | solution.py:158
  555.0 36.7 %copy-start.1 = (f32[32,128,128]{2,0,1:T(8,128)S(1)}, f32[32,128,128]{2,0,1:T(8,128)}, u32[]{:S(2)}) copy-start(f32[32,128,128]{2,0,1:T(8,128)} %get-tuple-element.24) | copy-start | bytes 6291460
  586.6 14.1 %copy-start.3 = (f32[32,128,128]{2,0,1:T(8,128)S(1)}, f32[32,128,128]{2,0,1:T(8,128)}, u32[]{:S(2)}) copy-start(f32[32,128,128]{2,0,1:T(8,128)} %get-tuple-element.22) | copy-start | bytes 6291460
  606.1 85.5 %all-reduce.14.cloned.1.call-start = ((), (), s32[]{:S(2)}) async-start(), calls=%async_computation.14 | async-start | bytes 262144
  607.1 298.4 %reduce-scatter.14.cloned.1.call-start = ((), (), s32[]{:S(2)}) async-start(), calls=%async_computation.12 | async-start | bytes 73728 | tf_op jit(solution)/shard_map/reduce_scatter | solution.py:158
  824.8 36.7 %copy-start.2 = (f32[32,128,128]{2,0,1:T(8,128)S(1)}, f32[32,128,128]{2,0,1:T(8,128)}, u32[]{:S(2)}) copy-start(f32[32,128,128]{2,0,1:T(8,128)} %get-tuple-element.24) | copy-start | bytes 6291460
  856.4 14.1 %copy-start.4 = (f32[32,128,128]{2,0,1:T(8,128)S(1)}, f32[32,128,128]{2,0,1:T(8,128)}, u32[]{:S(2)}) copy-start(f32[32,128,128]{2,0,1:T(8,128)} %get-tuple-element.22) | copy-start | bytes 6291460
  875.9 85.8 %all-reduce.16.cloned.1.call-start = ((), (), s32[]{:S(2)}) async-start(), calls=%async_computation.15 | async-start | bytes 262144
Sparse Core Ops, SparseCore 0:
  106.5 31.6 reduce-scatter.5
  194.1 29.1 reduce-scatter.7
  335.2 30.6 reduce-scatter.9
  606.3 29.3 reduce-scatter.11
  876.1 29.3 reduce-scatter.13
Sparse Core Ops, SparseCore 1:
  197.7 83.7 all-reduce.17
  338.8 83.1 all-reduce.11
  609.8 81.8 all-reduce.13
  879.9 81.8 all-reduce.15
where the time goes:
time: 1050 us; the launch traced here: 1040 us
  blocking collectives  419 us (40%)
  waiting for transfers between devices  401 us (38%)
  matrix products  112 us (11%)
  local copies, waits for them, and re-layouts  47.5 us (5%)
  between operations  23.6 us (2%)
  starting transfers between devices  22.4 us (2%)
  other arithmetic  14.1 us (1%)
    unnamed x13, waiting for transfers between devices  227 us
    psum x3, blocking collectives, precond_inner(): return lax.psum(jnp.sum(left * right), ('row', 'col'))  191 us
    psum x2, blocking collectives, shards(): lax.psum(jnp.sum(direction * image), ('row', 'col'))  132 us
    reduce_scatter x3, waiting for transfers between devices, shards(): lax.psum_scatter(col_part, 'row', scatter_dimension=0, tiled=True)  87 us
    all_to_all x1, waiting for transfers between devices, shards(): lax.all_to_all(send_blocks, 'col', split_axis=0, concat_axis=0, tiled=True)  63.6 us
    all_gather x3, blocking collectives, shards(): row_field = lax.all_gather(direction, 'col', axis=0, tiled=True)  53.9 us
    all_gather x3, blocking collectives, shards(): col_field = lax.all_gather(direction, 'row', axis=0, tiled=True)  42 us
    dot_general x2, matrix products, form_terms(): jnp.einsum('xhb,xhu->xbu', first_image, row_scale_factors(track_coefficie...  26.1 us
  transfers between devices with their start and end apart: 12, of which 9 were waited for; matrix products, arithmetic and copies ran while one was open for 10% of the time, Pallas kernels for 0%

commit v1 on v0

v1 whole, which is shorter than its diff:
```python
import jax
import jax.numpy as jnp
from jax import lax
from jax.experimental import pallas as pl
from jax.experimental.pallas import tpu as pltpu
from jax.sharding import PartitionSpec as P

ITERS = 3
N_ROW = 8
N_COL = 16
BLOCKS = 32
IMG = 16
IMG_ROW = N_COL * IMG
IMG_COL = N_ROW * IMG
LANES = 128
TRACKS = 1024
STEP = 2
CAP = 3
SLOT = 8
SENT = 4
SLOTS = N_COL * SLOT
PHASES = 3 + 1 + 6 * ITERS
MESH = pl.DeviceIdType.MESH
F32 = jnp.float32
BF16 = jnp.bfloat16


def dot(left, right):
    return jnp.dot(left, right, preferred_element_type=F32)


def halves(value):
    high = value.astype(BF16)
    low = (value - high.astype(F32)).astype(BF16)
    return high, low


def hot_dot(hot, value):
    both = dot(hot, jnp.concatenate(halves(value), axis=1))
    return both[:, 0:LANES] + both[:, LANES : 2 * LANES]


def iota(shape, axis):
    return lax.broadcasted_iota(jnp.int32, shape, axis).astype(F32)


def column_of(row_vector):
    n = row_vector.shape[1]
    return jnp.sum(
        jnp.where(iota((n, n), 0) == iota((n, n), 1), row_vector, 0.0), axis=1, keepdims=True
    )


def fold(value):
    return jnp.sum(value, axis=0, keepdims=True)


def total_of(value):
    return jnp.sum(value, axis=(0, 1), keepdims=True)


def spread_row(row):
    tile = jnp.broadcast_to(row, (16, TRACKS)).astype(BF16)
    return jnp.concatenate([tile] * 8, axis=0)


def block_terms(jac0, jac1, rad, resid, damp):
    h0, h1 = rad[0:1, :], rad[1:2, :]
    e0, e1 = resid[0:1, :], resid[1:2, :]
    inverse = 1.0 / (h0 * h0 + h1 * h1 + damp)
    grad = (h0 * e0 + h1 * e1) * inverse
    coef0 = spread_row(1.0 - h0 * h0 * inverse)
    coef1 = spread_row(1.0 - h1 * h1 * inverse)
    coef2 = spread_row(-h0 * h1 * inverse)
    coef3 = jnp.broadcast_to(e0 - h0 * grad, (16, TRACKS)).astype(BF16)
    coef4 = jnp.broadcast_to(e1 - h1 * grad, (16, TRACKS)).astype(BF16)
    jac0_t, jac1_t = jac0.T, jac1.T
    first = dot(jnp.concatenate([coef0 * jac0_t, coef3], axis=0), jac0)
    second = dot(jnp.concatenate([coef1 * jac1_t, coef4], axis=0), jac1)
    first, second = first.astype(BF16), second.astype(BF16)
    block_a, vector_a = first[0:128], first[128:144]
    block_b, vector_b = second[0:128], second[128:144]
    eye = iota((LANES, LANES), 0) == iota((LANES, LANES), 1)
    diag_a = fold(jnp.where(eye, block_a.astype(F32), 0.0))
    diag_b = fold(jnp.where(eye, block_b.astype(F32), 0.0))
    terms_a = jnp.concatenate([vector_a.astype(F32)[0:1], diag_a], axis=1)
    terms_b = jnp.concatenate([vector_b.astype(F32)[0:1], diag_b], axis=1)
    return block_a, block_b, coef2 * jac1_t, terms_a, terms_b


def kernel(
    jac_hbm,
    rad_hbm,
    resid_hbm,
    track_hbm,
    damp_ref,
    column_ref,
    slot_ref,
    rows_ref,
    cols_ref,
    state_ref,
    jac_ref,
    rad_ref,
    resid_ref,
    track_ref,
    weight_a,
    weight_b,
    weight_c,
    cross_ref,
    terms_a,
    terms_b,
    index_src,
    index_buf,
    rhs_b_src,
    rhs_b_buf,
    rhs_a_src,
    rhs_a_buf,
    rhs_r_src,
    rhs_r_buf,
    near_src,
    near_buf,
    field_src,
    field_buf,
    pick_src,
    pick_buf,
    prod_src,
    prod_buf,
    part_a_src,
    part_a_buf,
    part_b_src,
    part_b_buf,
    left_buf,
    load_sem,
    jac_sem,
    send_sem,
    recv_sem,
):
    row, col = lax.axis_index("row"), lax.axis_index("col")

    small = [
        pltpu.make_async_copy(src, dst, load_sem.at[i])
        for i, (src, dst) in enumerate(
            [(rad_hbm, rad_ref), (resid_hbm, resid_ref), (track_hbm, track_ref)]
        )
    ]
    for copy in small:
        copy.start()

    def load(step):
        part = pl.ds(step * STEP, STEP)
        return pltpu.make_async_copy(jac_hbm.at[part], jac_ref.at[part], jac_sem.at[step])

    def start_load(step, carry):
        load(step).start()
        return carry

    lax.fori_loop(0, BLOCKS // STEP, start_load, 0)

    for ref in (index_buf, rhs_b_buf, pick_buf, prod_buf):
        ref[...] = jnp.zeros_like(ref)

    barrier = pltpu.get_barrier_semaphore()

    col_hi, col_lo = lax.div(col, 4), lax.rem(col, 4)
    row_hi, row_lo = lax.div(row, 2), lax.rem(row, 2)
    col_steps = sorted(
        [(i, j) for i in range(4) for j in range(4) if i or j],
        key=lambda step: -sum(min(d, 4 - d) for d in step),
    )
    row_steps = [(i, j) for i in (2, 1, 3, 0) for j in (1, 0) if i or j]
    col_peers = [lax.rem(col_hi + i, 4) * 4 + lax.rem(col_lo + j, 4) for i, j in col_steps]
    row_peers = [lax.rem(row_hi + i, 4) * 2 + lax.rem(row_lo + j, 2) for i, j in row_steps]

    for peer in col_peers:
        pl.semaphore_signal(barrier, inc=1, device_id=(row, peer), device_id_type=MESH)
    for peer in row_peers:
        pl.semaphore_signal(barrier, inc=1, device_id=(peer, col), device_id_type=MESH)

    phases = iter(range(PHASES))
    pending = []

    def exchange(source, target, over_col, rows=None):
        phase = next(phases)
        peers, me = (col_peers, col) if over_col else (row_peers, row)
        rows = pl.ds(0, target.shape[1] if rows is None else rows)
        for peer in peers:
            pltpu.make_async_remote_copy(
                src_ref=source(peer).at[rows],
                dst_ref=target.at[me, rows],
                send_sem=send_sem.at[phase],
                recv_sem=recv_sem.at[phase],
                device_id=(row, peer) if over_col else (peer, col),
                device_id_type=MESH,
            ).start()
        whole = target.at[pl.ds(0, len(peers)), rows]
        copy = pltpu.make_async_remote_copy(
            src_ref=whole,
            dst_ref=whole,
            send_sem=send_sem.at[phase],
            recv_sem=recv_sem.at[phase],
            device_id=(row, peer) if over_col else (peer, col),
            device_id_type=MESH,
        )
        pending.append(copy)
        return copy

    def form(first, last):
        def one(step, carry):
            load(step).wait()
            for i in range(STEP):
                k = step * STEP + i
                block_a, block_b, cross, row_a, row_b = block_terms(
                    jac_ref[k, 0], jac_ref[k, 1], rad_ref[k], resid_ref[k], track_ref[pl.ds(k, 1), :]
                )
                at = pl.ds(pl.multiple_of(k * LANES, LANES), LANES)
                weight_a[at, 0:LANES] = block_a
                weight_b[at, :] = block_b
                cross_ref[k] = cross
                terms_a[pl.ds(k, 1), :] = row_a
                terms_b[pl.ds(k, 1), :] = row_b
            return carry

        lax.fori_loop(first // STEP, last // STEP, one, 0)

    def form_cross(first, last):
        def one(step, carry):
            for i in range(STEP):
                k = step * STEP + i
                at = pl.ds(pl.multiple_of(k * LANES, LANES), LANES)
                block_c = dot(cross_ref[k], jac_ref[k, 0]).astype(BF16)
                weight_c[at, :] = block_c
                weight_a[at, LANES : 2 * LANES] = block_c.T
            return carry

        lax.fori_loop(first // STEP, last // STEP, one, 0)

    for copy in small:
        copy.wait()
    form(0, 8)

    column_row = column_ref[...].astype(F32)
    slot_row = slot_ref[...].astype(F32)
    column = column_of(column_row)
    same = jnp.logical_and(
        column == column_row, iota((BLOCKS, BLOCKS), 1) < iota((BLOCKS, BLOCKS), 0)
    )
    place = jnp.sum(jnp.where(same, 1.0, 0.0), axis=1, keepdims=True)
    place_col = column * SLOT + place
    place_row = jnp.sum(
        jnp.where(iota((BLOCKS, BLOCKS), 0) == iota((BLOCKS, BLOCKS), 1), place_col, 0.0),
        axis=0,
        keepdims=True,
    )
    send_true = iota((SLOTS, BLOCKS), 0) == place_row
    send_hot = jnp.where(send_true, 1.0, 0.0).astype(BF16)
    take_hot = jnp.where(iota((BLOCKS, SLOTS), 1) == place_col, 1.0, 0.0).astype(BF16)
    slots_out = jnp.sum(jnp.where(send_true, slot_row + 1.0, 0.0), axis=1, keepdims=True) - 1.0
    index_src[...] = jnp.broadcast_to(slots_out, (SLOTS, LANES)).reshape(N_COL, SLOT, LANES)
    for j in range(N_COL):
        index_src[j, CAP : CAP + 1, 0:BLOCKS] = rows_ref[...].astype(F32)
    index_buf[col] = index_src[col]
    pl.semaphore_wait(barrier, N_COL + N_ROW - 2)
    copy = exchange(lambda peer: index_src.at[peer], index_buf, True, SENT)

    form(8, 24)

    copy.wait_recv()
    picked = iota((BLOCKS, LANES), 1) == column_of(slot_row)
    names_a = jnp.zeros((BLOCKS, LANES), F32)
    for j in range(N_COL):
        names_a = names_a + jnp.where(column == float(j), index_buf[j, CAP : CAP + 1, :], 0.0)
    key_a = jnp.sum(jnp.where(picked, names_a, 0.0), axis=1, keepdims=True)
    pick_a_true = jnp.where(iota((BLOCKS, IMG_ROW), 1) == key_a, 1.0, 0.0)
    pick_a = pick_a_true.astype(BF16)
    place_a = (
        jnp.concatenate([pick_a_true, jnp.zeros((LANES - BLOCKS, IMG_ROW), F32)], axis=0)
        .T.astype(BF16)
    )
    slots_in = index_buf[...].reshape(SLOTS, LANES)
    slot_lane = iota((SLOTS, LANES), 1)
    slot_sub = lax.broadcasted_iota(jnp.int32, (SLOTS, LANES), 0)
    used = jnp.logical_and(lax.rem(slot_sub, SLOT) < CAP, slots_in == slot_lane)
    cols_row = jnp.concatenate(
        [cols_ref[...].astype(F32), jnp.zeros((1, LANES - BLOCKS), F32)], axis=1
    )
    key_b = jnp.sum(jnp.where(used, cols_row + 1.0, 0.0), axis=1, keepdims=True) - 1.0
    pick_b_true = jnp.where(slot_lane == key_b, 1.0, 0.0)
    pick_b = pick_b_true.astype(BF16)
    place_b = pick_b_true.T.astype(BF16)
    scalar_rows = lax.rem(slot_sub, SLOT) == CAP

    form(24, 32)

    damping = damp_ref[...]
    pad_a = jnp.zeros((LANES - BLOCKS, 256), BF16)

    rhs_b_src[...] = dot(send_hot, terms_b[...].astype(BF16)).reshape(N_COL, SLOT, 256)
    rhs_b_buf[col] = rhs_b_src[col]
    copy_b = exchange(lambda peer: rhs_b_src.at[peer], rhs_b_buf, True, SENT)
    rhs_a_src[...] = dot(
        place_a, jnp.concatenate([terms_a[...].astype(BF16), pad_a], axis=0)
    ).reshape(N_COL, IMG, 256)
    rhs_a_buf[col] = rhs_a_src[col]
    copy_a = exchange(lambda peer: rhs_a_src.at[peer], rhs_a_buf, True)
    form_cross(0, 12)
    copy_b.wait_recv()
    rhs_r_src[...] = dot(place_b, rhs_b_buf[...].reshape(SLOTS, 256).astype(BF16)).reshape(
        N_ROW, IMG, 256
    )
    rhs_r_buf[row] = rhs_r_src[row]
    copy_r = exchange(lambda peer: rhs_r_src.at[peer], rhs_r_buf, False)
    form_cross(12, 22)
    copy_a.wait_recv()
    sums = jnp.sum(rhs_a_buf[...], axis=0)
    copy_r.wait_recv()
    sums = sums + jnp.sum(rhs_r_buf[...], axis=0)
    residual = sums[:, 0:LANES]
    diagonal = damping + sums[:, LANES:256]
    update = jnp.zeros_like(residual)

    row_in_left = lax.broadcasted_iota(jnp.int32, (2 * BLOCKS, LANES), 0)

    def spread(value, slot):
        stacked = jnp.concatenate(halves(value), axis=0)
        for k in range(BLOCKS):
            keep = jnp.logical_or(row_in_left == k, row_in_left == k + BLOCKS)
            left_buf[slot, :, k * LANES : (k + 1) * LANES] = jnp.where(
                keep, stacked, jnp.zeros_like(stacked)
            )

    def products(slot, weight):
        both = dot(left_buf[slot], weight[...])
        return both[0:BLOCKS] + both[BLOCKS : 2 * BLOCKS]

    own = dir_a = dir_b = prod_aa = prod_ca = prod_bb = prod_cb = inner_now = None
    for t in range(ITERS):
        scaled = residual / diagonal
        near_src[t, 0:IMG, :] = scaled
        near_src[t, IMG : IMG + 1, :] = fold(residual * scaled)
        near_buf[t, row] = near_src[t]
        copy_r = exchange(lambda peer: near_src.at[t], near_buf.at[t], False, IMG + 1)
        field_src[t] = scaled
        field_buf[t, col] = scaled
        copy_a = exchange(lambda peer: field_src.at[t], field_buf.at[t], True)

        if t == 0:
            form_cross(22, 32)
        copy_r.wait_recv()
        picks = hot_dot(pick_b, near_buf[t, :, 0:IMG, :].reshape(IMG_COL, LANES))
        norm = jnp.sum(near_buf[t, :, IMG : IMG + 1, :], axis=0)
        pick_src[t] = jnp.where(scalar_rows, norm, picks).reshape(N_COL, SLOT, LANES)
        pick_buf[t, col] = pick_src[t, col]
        copy_b = exchange(lambda peer: pick_src.at[t, peer], pick_buf.at[t], True, SENT)

        copy_a.wait_recv()
        field_a = hot_dot(pick_a, field_buf[t].reshape(IMG_ROW, LANES))
        spread(field_a, 0)
        from_a = products(0, weight_a)

        copy_b.wait_recv()
        received = pick_buf[t].reshape(SLOTS, LANES)
        field_b = hot_dot(take_hot, received)
        spread(field_b, 1)
        from_b = products(1, weight_b)
        inner_next = total_of(jnp.where(scalar_rows, received, 0.0))
        if t == 0:
            own, dir_a, dir_b = scaled, field_a, field_b
            prod_aa, prod_ca, prod_bb = from_a[:, 0:LANES], from_a[:, LANES:256], from_b
        else:
            ratio = inner_next / inner_now
            own = scaled + ratio * own
            dir_a = field_a + ratio * dir_a
            dir_b = field_b + ratio * dir_b
            prod_aa = from_a[:, 0:LANES] + ratio * prod_aa
            prod_ca = from_a[:, LANES:256] + ratio * prod_ca
            prod_bb = from_b + ratio * prod_bb
        inner_now = inner_next
        step_row = fold(dir_a * prod_aa + dir_b * (2.0 * prod_ca + prod_bb)) + fold(
            damping * own * own
        )
        sent = hot_dot(send_hot, prod_ca + prod_bb)
        prod_src[t] = jnp.where(scalar_rows, step_row, sent).reshape(N_COL, SLOT, LANES)
        prod_buf[t, col] = prod_src[t, col]
        copy_b = exchange(lambda peer: prod_src.at[t, peer], prod_buf.at[t], True, SENT)

        from_c = products(1, weight_c)
        prod_cb = from_c if t == 0 else from_c + ratio * prod_cb
        part = hot_dot(
            place_a,
            jnp.concatenate([prod_aa + prod_cb, jnp.zeros((LANES - BLOCKS, LANES), F32)], axis=0),
        )
        part_a_src[t] = part.reshape(N_COL, IMG, LANES)
        part_a_buf[t, col] = part_a_src[t, col]
        copy_a = exchange(lambda peer: part_a_src.at[t, peer], part_a_buf.at[t], True)

        copy_b.wait_recv()
        received = prod_buf[t].reshape(SLOTS, LANES)
        part = hot_dot(place_b, received)
        part_b_src[t, :, 0:IMG, :] = part.reshape(N_ROW, IMG, LANES)
        step_row = fold(jnp.where(scalar_rows, received, 0.0))
        part_b_src[t, :, IMG : IMG + 1, :] = jnp.broadcast_to(step_row, (N_ROW, 1, LANES))
        part_b_buf[t, row] = part_b_src[t, row]
        copy_r = exchange(lambda peer: part_b_src.at[t, peer], part_b_buf.at[t], False, IMG + 1)

        copy_a.wait_recv()
        image = damping * own + jnp.sum(part_a_buf[t], axis=0)
        copy_r.wait_recv()
        sums = jnp.sum(part_b_buf[t, :, 0 : IMG + 1, :], axis=0)
        image = image + sums[0:IMG]
        step_length = inner_now / total_of(sums[IMG : IMG + 1])
        if t < ITERS - 1:
            update = update + step_length * own
            residual = residual - step_length * image
    step = jnp.broadcast_to(step_length, own.shape)
    for i, value in enumerate([update, own, residual, image, step]):
        state_ref[i] = value
    for copy in pending:
        copy.wait_send()


def shards(
    obs_jac,
    rad_jac,
    obs_residual,
    track_damping,
    track_block_column,
    track_slot,
    pair_rows,
    pair_cols,
    image_damping,
):

    def both(*shape, dtype=F32):
        return [pltpu.VMEM(shape, dtype)] * 2

    scratch = [
        pltpu.VMEM(obs_jac.shape, BF16),
        pltpu.VMEM(rad_jac.shape, F32),
        pltpu.VMEM(obs_residual.shape, F32),
        pltpu.VMEM(track_damping.shape, F32),
        pltpu.VMEM((BLOCKS * LANES, 256), BF16),
        *both(BLOCKS * LANES, LANES, dtype=BF16),
        pltpu.VMEM((BLOCKS, LANES, TRACKS), BF16),
        *both(BLOCKS, 256),
        *both(N_COL, SLOT, LANES),
        *both(N_COL, SLOT, 256),
        *both(N_COL, IMG, 256),
        *both(N_ROW, IMG, 256),
        pltpu.VMEM((ITERS, IMG + 8, LANES), F32),
        pltpu.VMEM((ITERS, N_ROW, IMG + 8, LANES), F32),
        pltpu.VMEM((ITERS, IMG, LANES), F32),
        pltpu.VMEM((ITERS, N_COL, IMG, LANES), F32),
        *both(ITERS, N_COL, SLOT, LANES),
        *both(ITERS, N_COL, SLOT, LANES),
        *both(ITERS, N_COL, IMG, LANES),
        *both(ITERS, N_ROW, IMG + 8, LANES),
        pltpu.VMEM((2, 2 * BLOCKS, BLOCKS * LANES), BF16),
        pltpu.SemaphoreType.DMA((3,)),
        pltpu.SemaphoreType.DMA((BLOCKS // STEP,)),
        pltpu.SemaphoreType.DMA((PHASES,)),
        pltpu.SemaphoreType.DMA((PHASES,)),
    ]
    hbm = pl.BlockSpec(memory_space=pltpu.HBM)
    vmem = pl.BlockSpec(memory_space=pltpu.VMEM)
    state = (
        pl.pallas_call(
            kernel,
            out_shape=jax.ShapeDtypeStruct((5, IMG, LANES), F32),
            in_specs=[hbm] * 4 + [vmem] * 5,
            out_specs=vmem,
            scratch_shapes=scratch,
            compiler_params=pltpu.CompilerParams(
                collective_id=0, has_side_effects=True, vmem_limit_bytes=56 * 1024 * 1024
            ),
        )(
            obs_jac,
            rad_jac,
            obs_residual,
            track_damping,
            image_damping,
            track_block_column.reshape(1, BLOCKS),
            track_slot.reshape(1, BLOCKS),
            pair_rows.reshape(1, BLOCKS),
            pair_cols.reshape(1, BLOCKS),
        )
    )
    return state[0] + state[4] * state[1], state[2] - state[4] * state[3]


def solution(mesh):
    in_specs = (
        P(("row", "col"), None, None, None),
        P(("row", "col"), None, None),
        P(("row", "col"), None, None),
        P(("row", "col"), None),
        P(("row", "col"), None),
        P(("row", "col")),
        P(("row", "col")),
        P(("row", "col")),
        P(("row", "col"), None),
    )
    out_specs = (P(("row", "col"), None), P(("row", "col"), None))
    return jax.shard_map(shards, mesh=mesh, in_specs=in_specs, out_specs=out_specs, check_vma=False)
```

time: 1050 us -> 81.7 us (0.08)
  blocking collectives: 419 us -> 0 us
  waiting for transfers between devices: 401 us -> 0 us
  matrix products: 112 us -> 0 us
  Pallas kernels: 0 us -> 79.4 us
  local copies, waits for them, and re-layouts: 47.5 us -> 0 us
  between operations: 23.6 us -> 0.64 us
  starting transfers between devices: 22.4 us -> 0 us
  other arithmetic: 14.1 us -> 1.37 us
    psum x5 -> x0, blocking collectives: 323 us -> none  [the longest x3 191 us: precond_inner(): return lax.psum(jnp.sum(left * right), ('row', 'col'))]
    unnamed x13 -> x0, waiting for transfers between devices: 227 us -> none
    dot_general x34 -> x0, matrix products: 112 us -> none  [the longest x2 26.1 us: form_terms(): jnp.einsum('xhb,xhu->xbu', first_image, row_scale_factors(track_coefficie...]
    reduce_scatter x5 -> x0, waiting for transfers between devices: 111 us -> none  [the longest x3 87 us: shards(): lax.psum_scatter(col_part, 'row', scatter_dimension=0, tiled=True)]
    all_gather x6 -> x0, blocking collectives: 95.9 us -> none  [the longest x3 53.9 us: shards(): row_field = lax.all_gather(direction, 'col', axis=0, tiled=True)]
    pallas_call x0 -> x1, Pallas kernels: none -> 79.4 us  [shards(): pl.pallas_call(kernel, out_shape=jax.ShapeDtypeStruct((5, IMG, LANES), F3...]
    all_to_all x3 -> x0, waiting for transfers between devices: 63.6 us -> none  [the longest x1 63.6 us: shards(): lax.all_to_all(send_blocks, 'col', split_axis=0, concat_axis=0, tiled=True)]
    all_to_all x3 -> x0, starting transfers between devices: 21.8 us -> none  [the longest x1 8.43 us: shards(): lax.all_to_all(send_slots, 'col', split_axis=0, concat_axis=0, tiled=True)]
  transfers between devices with their start and end apart: 12 -> 0, of which waited for: 9 -> 0; matrix products, arithmetic and copies ran while one was open for 10% -> 0% of each run, Pallas kernels for 0% -> 0%
where the time goes in v1:
time: 81.7 us; the launch traced here: 81.5 us
  Pallas kernels  79.4 us (97%)
  other arithmetic  1.37 us (2%)
    pallas_call x1, Pallas kernels, shards(): pl.pallas_call(kernel, out_shape=jax.ShapeDtypeStruct((5, IMG, LANES), F3...  79.4 us

profile of v1, /device:TPU:1, one launch (start us, length us, event | category | flops | bytes accessed | tf_op | source)
XLA Modules:
  0.0 81.5 jit_solution(9982540886617781460)
XLA Ops:
  0.6 79.4 %shard_map.104 = f32[5,16,128]{2,1,0:T(8,128)} custom-call(bf16[32,2,1024,128]{3,2,1,0:T(8,128)(2,1)} %jac_hbm.1, f32[32,2,1024]{2,1,0:T(2,128)} %rad_hbm.1, f32[32,2,1024]{2,1,0:T(2,128)} %resid_hbm.1, f32[32,1024]{1,0:T(8,128)} %track_hbm.1, f32[16,128]{1,0:T(8,128)} %damp_ref.1, s32[1,32]{1,0:T(1,128)} %bitcast.8, s32[1,32]{1,0:T(1,128)} %bitcast.9, ...), custom_call_target="tpu_custom_call" | custom-call | tf_op jit(solution)/shard_map/pallas_call | solution.py:466
  80.1 1.4 %subtract_bitcast_fusion = (f32[16,128]{1,0:T(8,128)}, f32[16,128]{1,0:T(8,128)}) fusion(f32[5,16,128]{2,1,0:T(8,128)} %shard_map.104), kind=kLoop, calls=%fused_computation | loop fusion | flops 8192 | bytes 57344 | tf_op jit(solution)/shard_map/sub | solution.py:487

commit v2 on v1

--- a/solution.py
+++ b/solution.py
@@ -207,11 +207,14 @@
     def form(first, last):
         def one(step, carry):
             load(step).wait()
-            for i in range(STEP):
-                k = step * STEP + i
-                block_a, block_b, cross, row_a, row_b = block_terms(
+            blocks = [step * STEP + i for i in range(STEP)]
+            formed = [
+                block_terms(
                     jac_ref[k, 0], jac_ref[k, 1], rad_ref[k], resid_ref[k], track_ref[pl.ds(k, 1), :]
                 )
+                for k in blocks
+            ]
+            for k, (block_a, block_b, cross, row_a, row_b) in zip(blocks, formed):
                 at = pl.ds(pl.multiple_of(k * LANES, LANES), LANES)
                 weight_a[at, 0:LANES] = block_a
                 weight_b[at, :] = block_b
@@ -224,15 +227,16 @@
 
     def form_cross(first, last):
         def one(step, carry):
-            for i in range(STEP):
-                k = step * STEP + i
+            blocks = [step * 4 + i for i in range(4)]
+            formed = [dot(cross_ref[k], jac_ref[k, 0]).astype(BF16) for k in blocks]
+            formed = [(block_c, block_c.T) for block_c in formed]
+            for k, (block_c, block_c_t) in zip(blocks, formed):
                 at = pl.ds(pl.multiple_of(k * LANES, LANES), LANES)
-                block_c = dot(cross_ref[k], jac_ref[k, 0]).astype(BF16)
                 weight_c[at, :] = block_c
-                weight_a[at, LANES : 2 * LANES] = block_c.T
+                weight_a[at, LANES : 2 * LANES] = block_c_t
             return carry
 
-        lax.fori_loop(first // STEP, last // STEP, one, 0)
+        lax.fori_loop(first // 4, last // 4, one, 0)
 
     for copy in small:
         copy.wait()
@@ -309,7 +313,7 @@
     )
     rhs_r_buf[row] = rhs_r_src[row]
     copy_r = exchange(lambda peer: rhs_r_src.at[peer], rhs_r_buf, False)
-    form_cross(12, 22)
+    form_cross(12, 24)
     copy_a.wait_recv()
     sums = jnp.sum(rhs_a_buf[...], axis=0)
     copy_r.wait_recv()
@@ -344,7 +348,7 @@
         copy_a = exchange(lambda peer: field_src.at[t], field_buf.at[t], True)
 
         if t == 0:
-            form_cross(22, 32)
+            form_cross(24, 32)
         copy_r.wait_recv()
         picks = hot_dot(pick_b, near_buf[t, :, 0:IMG, :].reshape(IMG_COL, LANES))
         norm = jnp.sum(near_buf[t, :, IMG : IMG + 1, :], axis=0)

time: 81.7 us -> 81.7 us (level)
  no operation moved by 1% of the time
where the time goes in v2:
time: 81.7 us; the launch traced here: 81.5 us
  Pallas kernels  79.4 us (97%)
  other arithmetic  1.37 us (2%)
    pallas_call x1, Pallas kernels, shards(): pl.pallas_call(kernel, out_shape=jax.ShapeDtypeStruct((5, IMG, LANES), F3...  79.4 us

profile of v2, /device:TPU:1, one launch (start us, length us, event | category | flops | bytes accessed | tf_op | source)
XLA Modules:
  0.0 81.5 jit_solution(7248668350283241354)
XLA Ops:
  0.6 79.4 %shard_map.104 = f32[5,16,128]{2,1,0:T(8,128)} custom-call(bf16[32,2,1024,128]{3,2,1,0:T(8,128)(2,1)} %jac_hbm.1, f32[32,2,1024]{2,1,0:T(2,128)} %rad_hbm.1, f32[32,2,1024]{2,1,0:T(2,128)} %resid_hbm.1, f32[32,1024]{1,0:T(8,128)} %track_hbm.1, f32[16,128]{1,0:T(8,128)} %damp_ref.1, s32[1,32]{1,0:T(1,128)} %bitcast.8, s32[1,32]{1,0:T(1,128)} %bitcast.9, ...), custom_call_target="tpu_custom_call" | custom-call | tf_op jit(solution)/shard_map/pallas_call | solution.py:470
  80.1 1.4 %subtract_bitcast_fusion = (f32[16,128]{1,0:T(8,128)}, f32[16,128]{1,0:T(8,128)}) fusion(f32[5,16,128]{2,1,0:T(8,128)} %shard_map.104), kind=kLoop, calls=%fused_computation | loop fusion | flops 8192 | bytes 57344 | tf_op jit(solution)/shard_map/sub | solution.py:491

commit v3 on v2

--- a/solution.py
+++ b/solution.py
@@ -130,6 +130,15 @@
     part_b_src,
     part_b_buf,
     left_buf,
+    send_hot,
+    take_hot,
+    pick_a,
+    place_a,
+    pick_b,
+    place_b,
+    vector_ref,
+    rows_state,
+    scalar_ref,
     load_sem,
     jac_sem,
     send_sem,
@@ -176,54 +185,49 @@
     for peer in row_peers:
         pl.semaphore_signal(barrier, inc=1, device_id=(peer, col), device_id_type=MESH)
 
-    phases = iter(range(PHASES))
-    pending = []
-
-    def exchange(source, target, over_col, rows=None):
-        phase = next(phases)
+    def send(phase, source, target, over_col, rows):
         peers, me = (col_peers, col) if over_col else (row_peers, row)
-        rows = pl.ds(0, target.shape[1] if rows is None else rows)
         for peer in peers:
             pltpu.make_async_remote_copy(
-                src_ref=source(peer).at[rows],
-                dst_ref=target.at[me, rows],
+                src_ref=source(peer).at[pl.ds(0, rows)],
+                dst_ref=target.at[me, pl.ds(0, rows)],
                 send_sem=send_sem.at[phase],
                 recv_sem=recv_sem.at[phase],
                 device_id=(row, peer) if over_col else (peer, col),
                 device_id_type=MESH,
             ).start()
-        whole = target.at[pl.ds(0, len(peers)), rows]
-        copy = pltpu.make_async_remote_copy(
+
+    def waiter(phase, target, over_col, rows):
+        peers = col_peers if over_col else row_peers
+        whole = target.at[pl.ds(0, len(peers)), pl.ds(0, rows)]
+        return pltpu.make_async_remote_copy(
             src_ref=whole,
             dst_ref=whole,
             send_sem=send_sem.at[phase],
             recv_sem=recv_sem.at[phase],
-            device_id=(row, peer) if over_col else (peer, col),
+            device_id=(row, peers[0]) if over_col else (peers[0], col),
             device_id_type=MESH,
         )
-        pending.append(copy)
-        return copy
-
-    def form(first, last):
-        def one(step, carry):
-            load(step).wait()
-            blocks = [step * STEP + i for i in range(STEP)]
-            formed = [
-                block_terms(
-                    jac_ref[k, 0], jac_ref[k, 1], rad_ref[k], resid_ref[k], track_ref[pl.ds(k, 1), :]
-                )
-                for k in blocks
-            ]
-            for k, (block_a, block_b, cross, row_a, row_b) in zip(blocks, formed):
-                at = pl.ds(pl.multiple_of(k * LANES, LANES), LANES)
-                weight_a[at, 0:LANES] = block_a
-                weight_b[at, :] = block_b
-                cross_ref[k] = cross
-                terms_a[pl.ds(k, 1), :] = row_a
-                terms_b[pl.ds(k, 1), :] = row_b
-            return carry
-
-        lax.fori_loop(first // STEP, last // STEP, one, 0)
+
+    def form(step, carry):
+        pl.when(step == 4)(send_index)
+        pl.when(step == 12)(read_index)
+        load(step).wait()
+        blocks = [step * STEP + i for i in range(STEP)]
+        formed = [
+            block_terms(
+                jac_ref[k, 0], jac_ref[k, 1], rad_ref[k], resid_ref[k], track_ref[pl.ds(k, 1), :]
+            )
+            for k in blocks
+        ]
+        for k, (block_a, block_b, cross, row_a, row_b) in zip(blocks, formed):
+            at = pl.ds(pl.multiple_of(k * LANES, LANES), LANES)
+            weight_a[at, 0:LANES] = block_a
+            weight_b[at, :] = block_b
+            cross_ref[k] = cross
+            terms_a[pl.ds(k, 1), :] = row_a
+            terms_b[pl.ds(k, 1), :] = row_b
+        return carry
 
     def form_cross(first, last):
         def one(step, carry):
@@ -238,89 +242,84 @@
 
         lax.fori_loop(first // 4, last // 4, one, 0)
 
+    def block_columns():
+        column_row = column_ref[...].astype(F32)
+        column = column_of(column_row)
+        same = jnp.logical_and(
+            column == column_row, iota((BLOCKS, BLOCKS), 1) < iota((BLOCKS, BLOCKS), 0)
+        )
+        return column, column * SLOT + jnp.sum(jnp.where(same, 1.0, 0.0), axis=1, keepdims=True)
+
+    def send_index():
+        column, place_col = block_columns()
+        place_row = fold(
+            jnp.where(iota((BLOCKS, BLOCKS), 0) == iota((BLOCKS, BLOCKS), 1), place_col, 0.0)
+        )
+        send_true = iota((SLOTS, BLOCKS), 0) == place_row
+        send_hot[...] = jnp.where(send_true, 1.0, 0.0).astype(BF16)
+        take_hot[...] = jnp.where(iota((BLOCKS, SLOTS), 1) == place_col, 1.0, 0.0).astype(BF16)
+        slot_row = slot_ref[...].astype(F32)
+        slots_out = jnp.sum(jnp.where(send_true, slot_row + 1.0, 0.0), axis=1, keepdims=True) - 1.0
+        index_src[...] = jnp.broadcast_to(slots_out, (SLOTS, LANES)).reshape(N_COL, SLOT, LANES)
+        for j in range(N_COL):
+            index_src[j, CAP : CAP + 1, 0:BLOCKS] = rows_ref[...].astype(F32)
+        index_buf[col] = index_src[col]
+        pl.semaphore_wait(barrier, N_COL + N_ROW - 2)
+        send(0, lambda peer: index_src.at[peer], index_buf, True, SENT)
+
+    def read_index():
+        waiter(0, index_buf, True, SENT).wait_recv()
+        column, _ = block_columns()
+        picked = iota((BLOCKS, LANES), 1) == column_of(slot_ref[...].astype(F32))
+        names_a = jnp.zeros((BLOCKS, LANES), F32)
+        for j in range(N_COL):
+            names_a = names_a + jnp.where(column == float(j), index_buf[j, CAP : CAP + 1, :], 0.0)
+        key_a = jnp.sum(jnp.where(picked, names_a, 0.0), axis=1, keepdims=True)
+        pick = jnp.where(iota((BLOCKS, IMG_ROW), 1) == key_a, 1.0, 0.0)
+        pick_a[...] = pick.astype(BF16)
+        pick = jnp.concatenate([pick, jnp.zeros((LANES - BLOCKS, IMG_ROW), F32)], axis=0)
+        place_a[...] = pick.T.astype(BF16)
+        slots_in = index_buf[...].reshape(SLOTS, LANES)
+        used = jnp.logical_and(lax.rem(slot_sub, SLOT) < CAP, slots_in == iota((SLOTS, LANES), 1))
+        cols_row = jnp.concatenate(
+            [cols_ref[...].astype(F32), jnp.zeros((1, LANES - BLOCKS), F32)], axis=1
+        )
+        key_b = jnp.sum(jnp.where(used, cols_row + 1.0, 0.0), axis=1, keepdims=True) - 1.0
+        pick = jnp.where(iota((SLOTS, LANES), 1) == key_b, 1.0, 0.0)
+        pick_b[...] = pick.astype(BF16)
+        place_b[...] = pick.T.astype(BF16)
+
+    slot_sub = lax.broadcasted_iota(jnp.int32, (SLOTS, LANES), 0)
+    scalar_rows = lax.rem(slot_sub, SLOT) == CAP
     for copy in small:
         copy.wait()
-    form(0, 8)
-
-    column_row = column_ref[...].astype(F32)
-    slot_row = slot_ref[...].astype(F32)
-    column = column_of(column_row)
-    same = jnp.logical_and(
-        column == column_row, iota((BLOCKS, BLOCKS), 1) < iota((BLOCKS, BLOCKS), 0)
-    )
-    place = jnp.sum(jnp.where(same, 1.0, 0.0), axis=1, keepdims=True)
-    place_col = column * SLOT + place
-    place_row = jnp.sum(
-        jnp.where(iota((BLOCKS, BLOCKS), 0) == iota((BLOCKS, BLOCKS), 1), place_col, 0.0),
-        axis=0,
-        keepdims=True,
-    )
-    send_true = iota((SLOTS, BLOCKS), 0) == place_row
-    send_hot = jnp.where(send_true, 1.0, 0.0).astype(BF16)
-    take_hot = jnp.where(iota((BLOCKS, SLOTS), 1) == place_col, 1.0, 0.0).astype(BF16)
-    slots_out = jnp.sum(jnp.where(send_true, slot_row + 1.0, 0.0), axis=1, keepdims=True) - 1.0
-    index_src[...] = jnp.broadcast_to(slots_out, (SLOTS, LANES)).reshape(N_COL, SLOT, LANES)
-    for j in range(N_COL):
-        index_src[j, CAP : CAP + 1, 0:BLOCKS] = rows_ref[...].astype(F32)
-    index_buf[col] = index_src[col]
-    pl.semaphore_wait(barrier, N_COL + N_ROW - 2)
-    copy = exchange(lambda peer: index_src.at[peer], index_buf, True, SENT)
-
-    form(8, 24)
-
-    copy.wait_recv()
-    picked = iota((BLOCKS, LANES), 1) == column_of(slot_row)
-    names_a = jnp.zeros((BLOCKS, LANES), F32)
-    for j in range(N_COL):
-        names_a = names_a + jnp.where(column == float(j), index_buf[j, CAP : CAP + 1, :], 0.0)
-    key_a = jnp.sum(jnp.where(picked, names_a, 0.0), axis=1, keepdims=True)
-    pick_a_true = jnp.where(iota((BLOCKS, IMG_ROW), 1) == key_a, 1.0, 0.0)
-    pick_a = pick_a_true.astype(BF16)
-    place_a = (
-        jnp.concatenate([pick_a_true, jnp.zeros((LANES - BLOCKS, IMG_ROW), F32)], axis=0)
-        .T.astype(BF16)
-    )
-    slots_in = index_buf[...].reshape(SLOTS, LANES)
-    slot_lane = iota((SLOTS, LANES), 1)
-    slot_sub = lax.broadcasted_iota(jnp.int32, (SLOTS, LANES), 0)
-    used = jnp.logical_and(lax.rem(slot_sub, SLOT) < CAP, slots_in == slot_lane)
-    cols_row = jnp.concatenate(
-        [cols_ref[...].astype(F32), jnp.zeros((1, LANES - BLOCKS), F32)], axis=1
-    )
-    key_b = jnp.sum(jnp.where(used, cols_row + 1.0, 0.0), axis=1, keepdims=True) - 1.0
-    pick_b_true = jnp.where(slot_lane == key_b, 1.0, 0.0)
-    pick_b = pick_b_true.astype(BF16)
-    place_b = pick_b_true.T.astype(BF16)
-    scalar_rows = lax.rem(slot_sub, SLOT) == CAP
-
-    form(24, 32)
+    lax.fori_loop(0, BLOCKS // STEP, form, 0)
 
     damping = damp_ref[...]
     pad_a = jnp.zeros((LANES - BLOCKS, 256), BF16)
 
-    rhs_b_src[...] = dot(send_hot, terms_b[...].astype(BF16)).reshape(N_COL, SLOT, 256)
+    rhs_b_src[...] = dot(send_hot[...], terms_b[...].astype(BF16)).reshape(N_COL, SLOT, 256)
     rhs_b_buf[col] = rhs_b_src[col]
-    copy_b = exchange(lambda peer: rhs_b_src.at[peer], rhs_b_buf, True, SENT)
+    send(1, lambda peer: rhs_b_src.at[peer], rhs_b_buf, True, SENT)
     rhs_a_src[...] = dot(
-        place_a, jnp.concatenate([terms_a[...].astype(BF16), pad_a], axis=0)
+        place_a[...], jnp.concatenate([terms_a[...].astype(BF16), pad_a], axis=0)
     ).reshape(N_COL, IMG, 256)
     rhs_a_buf[col] = rhs_a_src[col]
-    copy_a = exchange(lambda peer: rhs_a_src.at[peer], rhs_a_buf, True)
+    send(2, lambda peer: rhs_a_src.at[peer], rhs_a_buf, True, IMG)
     form_cross(0, 12)
-    copy_b.wait_recv()
-    rhs_r_src[...] = dot(place_b, rhs_b_buf[...].reshape(SLOTS, 256).astype(BF16)).reshape(
+    waiter(1, rhs_b_buf, True, SENT).wait_recv()
+    rhs_r_src[...] = dot(place_b[...], rhs_b_buf[...].reshape(SLOTS, 256).astype(BF16)).reshape(
         N_ROW, IMG, 256
     )
     rhs_r_buf[row] = rhs_r_src[row]
-    copy_r = exchange(lambda peer: rhs_r_src.at[peer], rhs_r_buf, False)
+    send(3, lambda peer: rhs_r_src.at[peer], rhs_r_buf, False, IMG)
     form_cross(12, 24)
-    copy_a.wait_recv()
+    waiter(2, rhs_a_buf, True, IMG).wait_recv()
     sums = jnp.sum(rhs_a_buf[...], axis=0)
-    copy_r.wait_recv()
+    waiter(3, rhs_r_buf, False, IMG).wait_recv()
     sums = sums + jnp.sum(rhs_r_buf[...], axis=0)
-    residual = sums[:, 0:LANES]
+    right_side = sums[:, 0:LANES]
     diagonal = damping + sums[:, LANES:256]
-    update = jnp.zeros_like(residual)
 
     row_in_left = lax.broadcasted_iota(jnp.int32, (2 * BLOCKS, LANES), 0)
 
@@ -336,90 +335,122 @@
         both = dot(left_buf[slot], weight[...])
         return both[0:BLOCKS] + both[BLOCKS : 2 * BLOCKS]
 
-    own = dir_a = dir_b = prod_aa = prod_ca = prod_bb = prod_cb = inner_now = None
-    for t in range(ITERS):
+    def exchanges(t):
+        return [
+            (4 + 6 * t, near_buf.at[t], False, IMG + 1),
+            (5 + 6 * t, field_buf.at[t], True, IMG),
+            (6 + 6 * t, pick_buf.at[t], True, SENT),
+            (7 + 6 * t, prod_buf.at[t], True, SENT),
+            (8 + 6 * t, part_a_buf.at[t], True, IMG),
+            (9 + 6 * t, part_b_buf.at[t], False, IMG + 1),
+        ]
+
+    def iteration(t, carry):
+        update, own, residual, image = (vector_ref[i] for i in range(4))
+        dir_a, dir_b, *prods = (rows_state[i] for i in range(6))
+        step_length, inner_now = scalar_ref[0, 0:1, :], scalar_ref[1, 0:1, :]
+        near, field, pick, prod, part_a, part_b = exchanges(t)
+        update = update + step_length * own
+        residual = residual - step_length * image
         scaled = residual / diagonal
         near_src[t, 0:IMG, :] = scaled
         near_src[t, IMG : IMG + 1, :] = fold(residual * scaled)
         near_buf[t, row] = near_src[t]
-        copy_r = exchange(lambda peer: near_src.at[t], near_buf.at[t], False, IMG + 1)
+        send(near[0], lambda peer: near_src.at[t], *near[1:])
         field_src[t] = scaled
         field_buf[t, col] = scaled
-        copy_a = exchange(lambda peer: field_src.at[t], field_buf.at[t], True)
-
-        if t == 0:
-            form_cross(24, 32)
-        copy_r.wait_recv()
-        picks = hot_dot(pick_b, near_buf[t, :, 0:IMG, :].reshape(IMG_COL, LANES))
+        send(field[0], lambda peer: field_src.at[t], *field[1:])
+        pl.when(t == 0)(lambda: form_cross(24, 32))
+
+        waiter(*near).wait_recv()
+        picks = hot_dot(pick_b[...], near_buf[t, :, 0:IMG, :].reshape(IMG_COL, LANES))
         norm = jnp.sum(near_buf[t, :, IMG : IMG + 1, :], axis=0)
         pick_src[t] = jnp.where(scalar_rows, norm, picks).reshape(N_COL, SLOT, LANES)
         pick_buf[t, col] = pick_src[t, col]
-        copy_b = exchange(lambda peer: pick_src.at[t, peer], pick_buf.at[t], True, SENT)
-
-        copy_a.wait_recv()
-        field_a = hot_dot(pick_a, field_buf[t].reshape(IMG_ROW, LANES))
+        send(pick[0], lambda peer: pick_src.at[t, peer], *pick[1:])
+
+        waiter(*field).wait_recv()
+        field_a = hot_dot(pick_a[...], field_buf[t].reshape(IMG_ROW, LANES))
         spread(field_a, 0)
         from_a = products(0, weight_a)
 
-        copy_b.wait_recv()
+        waiter(*pick).wait_recv()
         received = pick_buf[t].reshape(SLOTS, LANES)
-        field_b = hot_dot(take_hot, received)
+        field_b = hot_dot(take_hot[...], received)
         spread(field_b, 1)
         from_b = products(1, weight_b)
         inner_next = total_of(jnp.where(scalar_rows, received, 0.0))
-        if t == 0:
-            own, dir_a, dir_b = scaled, field_a, field_b
-            prod_aa, prod_ca, prod_bb = from_a[:, 0:LANES], from_a[:, LANES:256], from_b
-        else:
-            ratio = inner_next / inner_now
-            own = scaled + ratio * own
-            dir_a = field_a + ratio * dir_a
-            dir_b = field_b + ratio * dir_b
-            prod_aa = from_a[:, 0:LANES] + ratio * prod_aa
-            prod_ca = from_a[:, LANES:256] + ratio * prod_ca
-            prod_bb = from_b + ratio * prod_bb
-        inner_now = inner_next
+        ratio = jnp.where(t == 0, 0.0, inner_next / inner_now)
+        own = scaled + ratio * own
+        dir_a = field_a + ratio * dir_a
+        dir_b = field_b + ratio * dir_b
+        prod_aa, prod_ca, prod_bb, prod_cb = prods
+        prod_aa = from_a[:, 0:LANES] + ratio * prod_aa
+        prod_ca = from_a[:, LANES:256] + ratio * prod_ca
+        prod_bb = from_b + ratio * prod_bb
         step_row = fold(dir_a * prod_aa + dir_b * (2.0 * prod_ca + prod_bb)) + fold(
             damping * own * own
         )
-        sent = hot_dot(send_hot, prod_ca + prod_bb)
+        sent = hot_dot(send_hot[...], prod_ca + prod_bb)
         prod_src[t] = jnp.where(scalar_rows, step_row, sent).reshape(N_COL, SLOT, LANES)
         prod_buf[t, col] = prod_src[t, col]
-        copy_b = exchange(lambda peer: prod_src.at[t, peer], prod_buf.at[t], True, SENT)
-
-        from_c = products(1, weight_c)
-        prod_cb = from_c if t == 0 else from_c + ratio * prod_cb
+        send(prod[0], lambda peer: prod_src.at[t, peer], *prod[1:])
+
+        prod_cb = products(1, weight_c) + ratio * prod_cb
         part = hot_dot(
-            place_a,
+            place_a[...],
             jnp.concatenate([prod_aa + prod_cb, jnp.zeros((LANES - BLOCKS, LANES), F32)], axis=0),
         )
         part_a_src[t] = part.reshape(N_COL, IMG, LANES)
         part_a_buf[t, col] = part_a_src[t, col]
-        copy_a = exchange(lambda peer: part_a_src.at[t, peer], part_a_buf.at[t], True)
-
-        copy_b.wait_recv()
+        send(part_a[0], lambda peer: part_a_src.at[t, peer], *part_a[1:])
+
+        waiter(*prod).wait_recv()
         received = prod_buf[t].reshape(SLOTS, LANES)
-        part = hot_dot(place_b, received)
+        part = hot_dot(place_b[...], received)
         part_b_src[t, :, 0:IMG, :] = part.reshape(N_ROW, IMG, LANES)
         step_row = fold(jnp.where(scalar_rows, received, 0.0))
         part_b_src[t, :, IMG : IMG + 1, :] = jnp.broadcast_to(step_row, (N_ROW, 1, LANES))
         part_b_buf[t, row] = part_b_src[t, row]
-        copy_r = exchange(lambda peer: part_b_src.at[t, peer], part_b_buf.at[t], False, IMG + 1)
-
-        copy_a.wait_recv()
+        send(part_b[0], lambda peer: part_b_src.at[t, peer], *part_b[1:])
+
+        waiter(*part_a).wait_recv()
         image = damping * own + jnp.sum(part_a_buf[t], axis=0)
-        copy_r.wait_recv()
+        waiter(*part_b).wait_recv()
         sums = jnp.sum(part_b_buf[t, :, 0 : IMG + 1, :], axis=0)
         image = image + sums[0:IMG]
-        step_length = inner_now / total_of(sums[IMG : IMG + 1])
-        if t < ITERS - 1:
-            update = update + step_length * own
-            residual = residual - step_length * image
-    step = jnp.broadcast_to(step_length, own.shape)
-    for i, value in enumerate([update, own, residual, image, step]):
-        state_ref[i] = value
-    for copy in pending:
-        copy.wait_send()
+        step_length = inner_next / total_of(sums[IMG : IMG + 1])
+        for i, value in enumerate([update, own, residual, image]):
+            vector_ref[i] = value
+        for i, value in enumerate([dir_a, dir_b, prod_aa, prod_ca, prod_bb, prod_cb]):
+            rows_state[i] = value
+        scalar_ref[0] = jnp.broadcast_to(step_length, (8, LANES))
+        scalar_ref[1] = jnp.broadcast_to(inner_next, (8, LANES))
+        return carry
+
+    vector_ref[...] = jnp.zeros_like(vector_ref)
+    vector_ref[2] = right_side
+    rows_state[...] = jnp.zeros_like(rows_state)
+    scalar_ref[0] = jnp.zeros((8, LANES), F32)
+    scalar_ref[1] = jnp.ones((8, LANES), F32)
+    lax.fori_loop(0, ITERS, iteration, 0)
+    state_ref[0:4] = vector_ref[...]
+    state_ref[4] = jnp.broadcast_to(scalar_ref[0, 0:1, :], (IMG, LANES))
+
+    for sent in (
+        (0, index_buf, True, SENT),
+        (1, rhs_b_buf, True, SENT),
+        (2, rhs_a_buf, True, IMG),
+        (3, rhs_r_buf, False, IMG),
+    ):
+        waiter(*sent).wait_send()
+
+    def drain(t, carry):
+        for sent in exchanges(t):
+            waiter(*sent).wait_send()
+        return carry
+
+    lax.fori_loop(0, ITERS, drain, 0)
 
 
 def shards(
@@ -459,6 +490,14 @@
         *both(ITERS, N_COL, IMG, LANES),
         *both(ITERS, N_ROW, IMG + 8, LANES),
         pltpu.VMEM((2, 2 * BLOCKS, BLOCKS * LANES), BF16),
+        pltpu.VMEM((SLOTS, BLOCKS), BF16),
+        pltpu.VMEM((BLOCKS, SLOTS), BF16),
+        pltpu.VMEM((BLOCKS, IMG_ROW), BF16),
+        pltpu.VMEM((IMG_ROW, LANES), BF16),
+        *both(SLOTS, LANES, dtype=BF16),
+        pltpu.VMEM((4, IMG, LANES), F32),
+        pltpu.VMEM((6, BLOCKS, LANES), F32),
+        pltpu.VMEM((2, 8, LANES), F32),
         pltpu.SemaphoreType.DMA((3,)),
         pltpu.SemaphoreType.DMA((BLOCKS // STEP,)),
         pltpu.SemaphoreType.DMA((PHASES,)),

time: 81.7 us -> 81.8 us (level)
  no operation moved by 1% of the time
where the time goes in v3:
time: 81.8 us; the launch traced here: 81.6 us
  Pallas kernels  79.6 us (97%)
  other arithmetic  1.37 us (2%)
    pallas_call x1, Pallas kernels, shards(): pl.pallas_call(kernel, out_shape=jax.ShapeDtypeStruct((5, IMG, LANES), F3...  79.6 us

profile of v3, /device:TPU:1, one launch (start us, length us, event | category | flops | bytes accessed | tf_op | source)
XLA Modules:
  0.0 81.6 jit_solution(9026496536013537626)
XLA Ops:
  0.6 79.6 %shard_map.104 = f32[5,16,128]{2,1,0:T(8,128)} custom-call(bf16[32,2,1024,128]{3,2,1,0:T(8,128)(2,1)} %jac_hbm.1, f32[32,2,1024]{2,1,0:T(2,128)} %rad_hbm.1, f32[32,2,1024]{2,1,0:T(2,128)} %resid_hbm.1, f32[32,1024]{1,0:T(8,128)} %track_hbm.1, f32[16,128]{1,0:T(8,128)} %damp_ref.1, s32[1,32]{1,0:T(1,128)} %bitcast.8, s32[1,32]{1,0:T(1,128)} %bitcast.9, ...), custom_call_target="tpu_custom_call" | custom-call | tf_op jit(solution)/shard_map/pallas_call | solution.py:509
  80.2 1.4 %subtract_bitcast_fusion = (f32[16,128]{1,0:T(8,128)}, f32[16,128]{1,0:T(8,128)}) fusion(f32[5,16,128]{2,1,0:T(8,128)} %shard_map.104), kind=kLoop, calls=%fused_computation | loop fusion | flops 8192 | bytes 57344 | tf_op jit(solution)/shard_map/sub | solution.py:530

commit v4 on v3

--- a/solution.py
+++ b/solution.py
@@ -19,7 +19,7 @@
 SLOT = 8
 SENT = 4
 SLOTS = N_COL * SLOT
-PHASES = 3 + 1 + 6 * ITERS
+PHASES = 5 + 8 * ITERS
 MESH = pl.DeviceIdType.MESH
 F32 = jnp.float32
 BF16 = jnp.bfloat16
@@ -115,6 +115,8 @@
     rhs_b_buf,
     rhs_a_src,
     rhs_a_buf,
+    rhs_m_src,
+    rhs_m_buf,
     rhs_r_src,
     rhs_r_buf,
     near_src,
@@ -127,6 +129,8 @@
     prod_buf,
     part_a_src,
     part_a_buf,
+    part_m_src,
+    part_m_buf,
     part_b_src,
     part_b_buf,
     left_buf,
@@ -242,6 +246,31 @@
 
         lax.fori_loop(first // 4, last // 4, one, 0)
 
+    lo_group = [(lax.rem(col_lo + j, 4), (row, col_hi * 4 + lax.rem(col_lo + j, 4))) for j in (2, 1, 3)]
+    hi_group = [(lax.rem(col_hi + i, 4), (row, lax.rem(col_hi + i, 4) * 4 + col_lo)) for i in (2, 1, 3)]
+    slab = pl.ds(col_hi * 4, 4)
+
+    def relay(phase, group, source, target):
+        for index, device in group:
+            pltpu.make_async_remote_copy(
+                src_ref=source(index),
+                dst_ref=target,
+                send_sem=send_sem.at[phase],
+                recv_sem=recv_sem.at[phase],
+                device_id=device,
+                device_id_type=MESH,
+            ).start()
+
+    def relayed(phase, whole):
+        return pltpu.make_async_remote_copy(
+            src_ref=whole,
+            dst_ref=whole,
+            send_sem=send_sem.at[phase],
+            recv_sem=recv_sem.at[phase],
+            device_id=lo_group[0][1],
+            device_id_type=MESH,
+        )
+
     def block_columns():
         column_row = column_ref[...].astype(F32)
         column = column_of(column_row)
@@ -304,8 +333,8 @@
     rhs_a_src[...] = dot(
         place_a[...], jnp.concatenate([terms_a[...].astype(BF16), pad_a], axis=0)
     ).reshape(N_COL, IMG, 256)
-    rhs_a_buf[col] = rhs_a_src[col]
-    send(2, lambda peer: rhs_a_src.at[peer], rhs_a_buf, True, IMG)
+    rhs_a_buf[col_hi] = rhs_a_src[slab]
+    relay(2, hi_group, lambda i: rhs_a_src.at[pl.ds(i * 4, 4)], rhs_a_buf.at[col_hi])
     form_cross(0, 12)
     waiter(1, rhs_b_buf, True, SENT).wait_recv()
     rhs_r_src[...] = dot(place_b[...], rhs_b_buf[...].reshape(SLOTS, 256).astype(BF16)).reshape(
@@ -313,9 +342,13 @@
     )
     rhs_r_buf[row] = rhs_r_src[row]
     send(3, lambda peer: rhs_r_src.at[peer], rhs_r_buf, False, IMG)
+    relayed(2, rhs_a_buf.at[pl.ds(0, 3)]).wait_recv()
+    rhs_m_src[...] = jnp.sum(rhs_a_buf[...], axis=0)
+    rhs_m_buf[col_lo] = rhs_m_src[col_lo]
+    relay(4, lo_group, lambda j: rhs_m_src.at[j], rhs_m_buf.at[col_lo])
     form_cross(12, 24)
-    waiter(2, rhs_a_buf, True, IMG).wait_recv()
-    sums = jnp.sum(rhs_a_buf[...], axis=0)
+    relayed(4, rhs_m_buf.at[pl.ds(0, 3)]).wait_recv()
+    sums = jnp.sum(rhs_m_buf[...], axis=0)
     waiter(3, rhs_r_buf, False, IMG).wait_recv()
     sums = sums + jnp.sum(rhs_r_buf[...], axis=0)
     right_side = sums[:, 0:LANES]
@@ -336,20 +369,24 @@
         return both[0:BLOCKS] + both[BLOCKS : 2 * BLOCKS]
 
     def exchanges(t):
+        first = 5 + 8 * t
         return [
-            (4 + 6 * t, near_buf.at[t], False, IMG + 1),
-            (5 + 6 * t, field_buf.at[t], True, IMG),
-            (6 + 6 * t, pick_buf.at[t], True, SENT),
-            (7 + 6 * t, prod_buf.at[t], True, SENT),
-            (8 + 6 * t, part_a_buf.at[t], True, IMG),
-            (9 + 6 * t, part_b_buf.at[t], False, IMG + 1),
+            (first, near_buf.at[t], False, IMG + 1),
+            (first + 1, pick_buf.at[t], True, SENT),
+            (first + 2, prod_buf.at[t], True, SENT),
+            (first + 3, part_b_buf.at[t], False, IMG + 1),
+        ], [
+            (first + 4, field_buf.at[t, pl.ds(0, 3)]),
+            (first + 5, field_buf.at[t, pl.ds(0, 12)]),
+            (first + 6, part_a_buf.at[t, pl.ds(0, 3)]),
+            (first + 7, part_m_buf.at[t, pl.ds(0, 3)]),
         ]
 
     def iteration(t, carry):
         update, own, residual, image = (vector_ref[i] for i in range(4))
         dir_a, dir_b, *prods = (rows_state[i] for i in range(6))
         step_length, inner_now = scalar_ref[0, 0:1, :], scalar_ref[1, 0:1, :]
-        near, field, pick, prod, part_a, part_b = exchanges(t)
+        (near, pick, prod, part_b), (field_x, field_z, part_z, part_x) = exchanges(t)
         update = update + step_length * own
         residual = residual - step_length * image
         scaled = residual / diagonal
@@ -359,8 +396,10 @@
         send(near[0], lambda peer: near_src.at[t], *near[1:])
         field_src[t] = scaled
         field_buf[t, col] = scaled
-        send(field[0], lambda peer: field_src.at[t], *field[1:])
+        relay(field_x[0], lo_group, lambda j: field_src.at[t], field_buf.at[t, col])
         pl.when(t == 0)(lambda: form_cross(24, 32))
+        relayed(*field_x).wait_recv()
+        relay(field_z[0], hi_group, lambda i: field_buf.at[t, slab], field_buf.at[t, slab])
 
         waiter(*near).wait_recv()
         picks = hot_dot(pick_b[...], near_buf[t, :, 0:IMG, :].reshape(IMG_COL, LANES))
@@ -369,7 +408,7 @@
         pick_buf[t, col] = pick_src[t, col]
         send(pick[0], lambda peer: pick_src.at[t, peer], *pick[1:])
 
-        waiter(*field).wait_recv()
+        relayed(*field_z).wait_recv()
         field_a = hot_dot(pick_a[...], field_buf[t].reshape(IMG_ROW, LANES))
         spread(field_a, 0)
         from_a = products(0, weight_a)
@@ -402,8 +441,10 @@
             jnp.concatenate([prod_aa + prod_cb, jnp.zeros((LANES - BLOCKS, LANES), F32)], axis=0),
         )
         part_a_src[t] = part.reshape(N_COL, IMG, LANES)
-        part_a_buf[t, col] = part_a_src[t, col]
-        send(part_a[0], lambda peer: part_a_src.at[t, peer], *part_a[1:])
+        part_a_buf[t, col_hi] = part_a_src[t, slab]
+        relay(
+            part_z[0], hi_group, lambda i: part_a_src.at[t, pl.ds(i * 4, 4)], part_a_buf.at[t, col_hi]
+        )
 
         waiter(*prod).wait_recv()
         received = prod_buf[t].reshape(SLOTS, LANES)
@@ -414,8 +455,12 @@
         part_b_buf[t, row] = part_b_src[t, row]
         send(part_b[0], lambda peer: part_b_src.at[t, peer], *part_b[1:])
 
-        waiter(*part_a).wait_recv()
-        image = damping * own + jnp.sum(part_a_buf[t], axis=0)
+        relayed(*part_z).wait_recv()
+        part_m_src[t] = jnp.sum(part_a_buf[t], axis=0)
+        part_m_buf[t, col_lo] = part_m_src[t, col_lo]
+        relay(part_x[0], lo_group, lambda j: part_m_src.at[t, j], part_m_buf.at[t, col_lo])
+        relayed(*part_x).wait_recv()
+        image = damping * own + jnp.sum(part_m_buf[t], axis=0)
         waiter(*part_b).wait_recv()
         sums = jnp.sum(part_b_buf[t, :, 0 : IMG + 1, :], axis=0)
         image = image + sums[0:IMG]
@@ -440,14 +485,18 @@
     for sent in (
         (0, index_buf, True, SENT),
         (1, rhs_b_buf, True, SENT),
-        (2, rhs_a_buf, True, IMG),
         (3, rhs_r_buf, False, IMG),
     ):
         waiter(*sent).wait_send()
+    relayed(2, rhs_a_buf.at[pl.ds(0, 3)]).wait_send()
+    relayed(4, rhs_m_buf.at[pl.ds(0, 3)]).wait_send()
 
     def drain(t, carry):
-        for sent in exchanges(t):
+        whole, stages = exchanges(t)
+        for sent in whole:
             waiter(*sent).wait_send()
+        for sent in stages:
+            relayed(*sent).wait_send()
         return carry
 
     lax.fori_loop(0, ITERS, drain, 0)
@@ -479,7 +528,9 @@
         *both(BLOCKS, 256),
         *both(N_COL, SLOT, LANES),
         *both(N_COL, SLOT, 256),
-        *both(N_COL, IMG, 256),
+        pltpu.VMEM((N_COL, IMG, 256), F32),
+        pltpu.VMEM((4, 4, IMG, 256), F32),
+        *both(4, IMG, 256),
         *both(N_ROW, IMG, 256),
         pltpu.VMEM((ITERS, IMG + 8, LANES), F32),
         pltpu.VMEM((ITERS, N_ROW, IMG + 8, LANES), F32),
@@ -487,7 +538,9 @@
         pltpu.VMEM((ITERS, N_COL, IMG, LANES), F32),
         *both(ITERS, N_COL, SLOT, LANES),
         *both(ITERS, N_COL, SLOT, LANES),
-        *both(ITERS, N_COL, IMG, LANES),
+        pltpu.VMEM((ITERS, N_COL, IMG, LANES), F32),
+        pltpu.VMEM((ITERS, 4, 4, IMG, LANES), F32),
+        *both(ITERS, 4, IMG, LANES),
         *both(ITERS, N_ROW, IMG + 8, LANES),
         pltpu.VMEM((2, 2 * BLOCKS, BLOCKS * LANES), BF16),
         pltpu.VMEM((SLOTS, BLOCKS), BF16),

time: 81.8 us -> 82.6 us (level)
    pallas_call x1, Pallas kernels: 79.6 us -> 80.4 us  [shards(): pl.pallas_call(kernel, out_shape=jax.ShapeDtypeStruct((5, IMG, LANES), F3...]
where the time goes in v4:
time: 82.6 us; the launch traced here: 82.4 us
  Pallas kernels  80.4 us (97%)
  other arithmetic  1.37 us (2%)
    pallas_call x1, Pallas kernels, shards(): pl.pallas_call(kernel, out_shape=jax.ShapeDtypeStruct((5, IMG, LANES), F3...  80.4 us

profile of v4, /device:TPU:1, one launch (start us, length us, event | category | flops | bytes accessed | tf_op | source)
XLA Modules:
  0.0 82.4 jit_solution(12820810252929222882)
XLA Ops:
  0.6 80.4 %shard_map.104 = f32[5,16,128]{2,1,0:T(8,128)} custom-call(bf16[32,2,1024,128]{3,2,1,0:T(8,128)(2,1)} %jac_hbm.1, f32[32,2,1024]{2,1,0:T(2,128)} %rad_hbm.1, f32[32,2,1024]{2,1,0:T(2,128)} %resid_hbm.1, f32[32,1024]{1,0:T(8,128)} %track_hbm.1, f32[16,128]{1,0:T(8,128)} %damp_ref.1, s32[1,32]{1,0:T(1,128)} %bitcast.8, s32[1,32]{1,0:T(1,128)} %bitcast.9, ...), custom_call_target="tpu_custom_call" | custom-call | tf_op jit(solution)/shard_map/pallas_call | solution.py:562
  81.0 1.4 %subtract_bitcast_fusion = (f32[16,128]{1,0:T(8,128)}, f32[16,128]{1,0:T(8,128)}) fusion(f32[5,16,128]{2,1,0:T(8,128)} %shard_map.104), kind=kLoop, calls=%fused_computation | loop fusion | flops 8192 | bytes 57344 | tf_op jit(solution)/shard_map/sub | solution.py:583

commit v5 on v3

--- a/solution.py
+++ b/solution.py
@@ -16,6 +16,7 @@
 TRACKS = 1024
 STEP = 2
 CAP = 3
+AHEAD = 4
 SLOT = 8
 SENT = 4
 SLOTS = N_COL * SLOT
@@ -163,7 +164,7 @@
         load(step).start()
         return carry
 
-    lax.fori_loop(0, BLOCKS // STEP, start_load, 0)
+    lax.fori_loop(0, AHEAD, start_load, 0)
 
     for ref in (index_buf, rhs_b_buf, pick_buf, prod_buf):
         ref[...] = jnp.zeros_like(ref)
@@ -212,6 +213,7 @@
     def form(step, carry):
         pl.when(step == 4)(send_index)
         pl.when(step == 12)(read_index)
+        pl.when(step + AHEAD < BLOCKS // STEP)(lambda: load(step + AHEAD).start())
         load(step).wait()
         blocks = [step * STEP + i for i in range(STEP)]
         formed = [
@@ -316,6 +318,12 @@
     form_cross(12, 24)
     waiter(2, rhs_a_buf, True, IMG).wait_recv()
     sums = jnp.sum(rhs_a_buf[...], axis=0)
+    for sent in (
+        (0, index_buf, True, SENT),
+        (1, rhs_b_buf, True, SENT),
+        (2, rhs_a_buf, True, IMG),
+    ):
+        waiter(*sent).wait_send()
     waiter(3, rhs_r_buf, False, IMG).wait_recv()
     sums = sums + jnp.sum(rhs_r_buf[...], axis=0)
     right_side = sums[:, 0:LANES]
@@ -364,7 +372,7 @@
 
         waiter(*near).wait_recv()
         picks = hot_dot(pick_b[...], near_buf[t, :, 0:IMG, :].reshape(IMG_COL, LANES))
-        norm = jnp.sum(near_buf[t, :, IMG : IMG + 1, :], axis=0)
+        norm = total_of(jnp.sum(near_buf[t, :, IMG : IMG + 1, :], axis=0))
         pick_src[t] = jnp.where(scalar_rows, norm, picks).reshape(N_COL, SLOT, LANES)
         pick_buf[t, col] = pick_src[t, col]
         send(pick[0], lambda peer: pick_src.at[t, peer], *pick[1:])
@@ -379,7 +387,7 @@
         field_b = hot_dot(take_hot[...], received)
         spread(field_b, 1)
         from_b = products(1, weight_b)
-        inner_next = total_of(jnp.where(scalar_rows, received, 0.0))
+        inner_next = fold(jnp.where(scalar_rows, received, 0.0))
         ratio = jnp.where(t == 0, 0.0, inner_next / inner_now)
         own = scaled + ratio * own
         dir_a = field_a + ratio * dir_a
@@ -388,8 +396,8 @@
         prod_aa = from_a[:, 0:LANES] + ratio * prod_aa
         prod_ca = from_a[:, LANES:256] + ratio * prod_ca
         prod_bb = from_b + ratio * prod_bb
-        step_row = fold(dir_a * prod_aa + dir_b * (2.0 * prod_ca + prod_bb)) + fold(
-            damping * own * own
+        step_row = total_of(
+            fold(dir_a * prod_aa + dir_b * (2.0 * prod_ca + prod_bb)) + fold(damping * own * own)
         )
         sent = hot_dot(send_hot[...], prod_ca + prod_bb)
         prod_src[t] = jnp.where(scalar_rows, step_row, sent).reshape(N_COL, SLOT, LANES)
@@ -416,10 +424,12 @@
 
         waiter(*part_a).wait_recv()
         image = damping * own + jnp.sum(part_a_buf[t], axis=0)
+        for sent in (near, field, pick, prod, part_a):
+            waiter(*sent).wait_send()
         waiter(*part_b).wait_recv()
         sums = jnp.sum(part_b_buf[t, :, 0 : IMG + 1, :], axis=0)
         image = image + sums[0:IMG]
-        step_length = inner_next / total_of(sums[IMG : IMG + 1])
+        step_length = inner_next / sums[IMG : IMG + 1]
         for i, value in enumerate([update, own, residual, image]):
             vector_ref[i] = value
         for i, value in enumerate([dir_a, dir_b, prod_aa, prod_ca, prod_bb, prod_cb]):
@@ -437,17 +447,10 @@
     state_ref[0:4] = vector_ref[...]
     state_ref[4] = jnp.broadcast_to(scalar_ref[0, 0:1, :], (IMG, LANES))
 
-    for sent in (
-        (0, index_buf, True, SENT),
-        (1, rhs_b_buf, True, SENT),
-        (2, rhs_a_buf, True, IMG),
-        (3, rhs_r_buf, False, IMG),
-    ):
-        waiter(*sent).wait_send()
+    waiter(3, rhs_r_buf, False, IMG).wait_send()
 
     def drain(t, carry):
-        for sent in exchanges(t):
-            waiter(*sent).wait_send()
+        waiter(*exchanges(t)[-1]).wait_send()
         return carry
 
     lax.fori_loop(0, ITERS, drain, 0)

time: 81.8 us -> 81.5 us (level)
  no operation moved by 1% of the time
where the time goes in v5:
time: 81.5 us; the launch traced here: 81.3 us
  Pallas kernels  79.3 us (97%)
  other arithmetic  1.37 us (2%)
    pallas_call x1, Pallas kernels, shards(): pl.pallas_call(kernel, out_shape=jax.ShapeDtypeStruct((5, IMG, LANES), F3...  79.3 us

profile of v5, /device:TPU:1, one launch (start us, length us, event | category | flops | bytes accessed | tf_op | source)
XLA Modules:
  0.0 81.3 jit_solution(7307842441825716602)
XLA Ops:
  0.6 79.3 %shard_map.104 = f32[5,16,128]{2,1,0:T(8,128)} custom-call(bf16[32,2,1024,128]{3,2,1,0:T(8,128)(2,1)} %jac_hbm.1, f32[32,2,1024]{2,1,0:T(2,128)} %rad_hbm.1, f32[32,2,1024]{2,1,0:T(2,128)} %resid_hbm.1, f32[32,1024]{1,0:T(8,128)} %track_hbm.1, f32[16,128]{1,0:T(8,128)} %damp_ref.1, s32[1,32]{1,0:T(1,128)} %bitcast.8, s32[1,32]{1,0:T(1,128)} %bitcast.9, ...), custom_call_target="tpu_custom_call" | custom-call | tf_op jit(solution)/shard_map/pallas_call | solution.py:512
  79.9 1.4 %subtract_bitcast_fusion = (f32[16,128]{1,0:T(8,128)}, f32[16,128]{1,0:T(8,128)}) fusion(f32[5,16,128]{2,1,0:T(8,128)} %shard_map.104), kind=kLoop, calls=%fused_computation | loop fusion | flops 8192 | bytes 57344 | tf_op jit(solution)/shard_map/sub | solution.py:533

commit v6 on v5

--- a/solution.py
+++ b/solution.py
@@ -14,7 +14,7 @@
 IMG_COL = N_ROW * IMG
 LANES = 128
 TRACKS = 1024
-STEP = 2
+STEP = 4
 CAP = 3
 AHEAD = 4
 SLOT = 8
@@ -211,8 +211,8 @@
         )
 
     def form(step, carry):
-        pl.when(step == 4)(send_index)
-        pl.when(step == 12)(read_index)
+        pl.when(step == 2)(send_index)
+        pl.when(step == 6)(read_index)
         pl.when(step + AHEAD < BLOCKS // STEP)(lambda: load(step + AHEAD).start())
         load(step).wait()
         blocks = [step * STEP + i for i in range(STEP)]
@@ -308,14 +308,14 @@
     ).reshape(N_COL, IMG, 256)
     rhs_a_buf[col] = rhs_a_src[col]
     send(2, lambda peer: rhs_a_src.at[peer], rhs_a_buf, True, IMG)
-    form_cross(0, 12)
+    form_cross(0, 8)
     waiter(1, rhs_b_buf, True, SENT).wait_recv()
     rhs_r_src[...] = dot(place_b[...], rhs_b_buf[...].reshape(SLOTS, 256).astype(BF16)).reshape(
         N_ROW, IMG, 256
     )
     rhs_r_buf[row] = rhs_r_src[row]
     send(3, lambda peer: rhs_r_src.at[peer], rhs_r_buf, False, IMG)
-    form_cross(12, 24)
+    form_cross(8, 16)
     waiter(2, rhs_a_buf, True, IMG).wait_recv()
     sums = jnp.sum(rhs_a_buf[...], axis=0)
     for sent in (
@@ -368,7 +368,7 @@
         field_src[t] = scaled
         field_buf[t, col] = scaled
         send(field[0], lambda peer: field_src.at[t], *field[1:])
-        pl.when(t == 0)(lambda: form_cross(24, 32))
+        pl.when(t == 0)(lambda: form_cross(16, 24))
 
         waiter(*near).wait_recv()
         picks = hot_dot(pick_b[...], near_buf[t, :, 0:IMG, :].reshape(IMG_COL, LANES))
@@ -377,6 +377,7 @@
         pick_buf[t, col] = pick_src[t, col]
         send(pick[0], lambda peer: pick_src.at[t, peer], *pick[1:])
 
+        pl.when(t == 0)(lambda: form_cross(24, 32))
         waiter(*field).wait_recv()
         field_a = hot_dot(pick_a[...], field_buf[t].reshape(IMG_ROW, LANES))
         spread(field_a, 0)

time: 81.5 us -> 80.6 us (0.989)
  Pallas kernels: 79.3 us -> 78.3 us
    pallas_call x1, Pallas kernels: 79.3 us -> 78.3 us  [shards(): pl.pallas_call(kernel, out_shape=jax.ShapeDtypeStruct((5, IMG, LANES), F3...]
where the time goes in v6:
time: 80.6 us; the launch traced here: 80.4 us
  Pallas kernels  78.3 us (97%)
  other arithmetic  1.37 us (2%)
    pallas_call x1, Pallas kernels, shards(): pl.pallas_call(kernel, out_shape=jax.ShapeDtypeStruct((5, IMG, LANES), F3...  78.3 us

profile of v6, /device:TPU:1, one launch (start us, length us, event | category | flops | bytes accessed | tf_op | source)
XLA Modules:
  0.0 80.4 jit_solution(9620701546675876384)
XLA Ops:
  0.6 78.3 %shard_map.104 = f32[5,16,128]{2,1,0:T(8,128)} custom-call(bf16[32,2,1024,128]{3,2,1,0:T(8,128)(2,1)} %jac_hbm.1, f32[32,2,1024]{2,1,0:T(2,128)} %rad_hbm.1, f32[32,2,1024]{2,1,0:T(2,128)} %resid_hbm.1, f32[32,1024]{1,0:T(8,128)} %track_hbm.1, f32[16,128]{1,0:T(8,128)} %damp_ref.1, s32[1,32]{1,0:T(1,128)} %bitcast.8, s32[1,32]{1,0:T(1,128)} %bitcast.9, ...), custom_call_target="tpu_custom_call" | custom-call | tf_op jit(solution)/shard_map/pallas_call | solution.py:513
  79.0 1.4 %subtract_bitcast_fusion = (f32[16,128]{1,0:T(8,128)}, f32[16,128]{1,0:T(8,128)}) fusion(f32[5,16,128]{2,1,0:T(8,128)} %shard_map.104), kind=kLoop, calls=%fused_computation | loop fusion | flops 8192 | bytes 57344 | tf_op jit(solution)/shard_map/sub | solution.py:534
